TPU v7x, 32 devices: a whole 2x2x4 slice. The times are simulated.
32 devices in a mesh: blk: 16 (over z, y, core), head: 2 (over x).
Axes of the slice: x: 2, y: 2, z: 4, core: 2. Of those that a mesh axis runs over, the one named last changes fastest.
Arguments:
- queries: bfloat16 [1024, 3584], P('blk', 'head'), may hold values from -64 to 64
- new_keys: bfloat16 [1024, 3584], P('blk', 'head'), may hold values from -6 to 6
- new_values: bfloat16 [1024, 3584], P('blk', 'head'), may hold values from -6 to 6
- key_cache: bfloat16 [128, 128, 3584], P('blk', None, 'head'), may hold values from -6 to 6
- value_cache: bfloat16 [128, 128, 3584], P('blk', None, 'head'), may hold values from -6 to 6
- out_weight: bfloat16 [3584, 3584], P('head'), may hold values from -0.09375 to 0.09375
- cache_len: int32 [1], replicated, may hold values from 1 to 16384, as said below
- page_table: int32 [128], replicated, may hold values from 0 to 127, each once
- block_perm: int32 [16], replicated, may hold values from 0 to 15, each once
Outputs:
- projected: bfloat16 [1024, 3584], P('blk', 'head')
Inputs may be any that keep to these rules, and one draw needn't show every extreme that they name: `cache_len`: some request has exactly 16384 cached tokens. `page_table`: each global page appears once. `block_perm`: each query block appears once.
All inputs are finite; a program needn't handle non-finite values.
Results may differ from a plain program's by a relative error of at most 0.015.
Values may be sent and summed in bfloat16 or wider, within the bound.
A program may use at most 128 MiB of HBM per device.

v0:
```python
import math

import jax
import jax.numpy as jnp
from jax import lax
from jax.sharding import PartitionSpec as P

HD = 224
PAGE = 128
P_DEV = 8
NEW = 1024
TOK_DEV = 64
MAXP = 128


def block_partial(query_rows, key_rows, value_rows, visible):
    head_count = query_rows.shape[1] // HD
    query_heads = query_rows.reshape(query_rows.shape[0], head_count, HD)
    key_heads = key_rows.reshape(key_rows.shape[0], head_count, HD)
    value_heads = value_rows.reshape(value_rows.shape[0], head_count, HD)
    scores = jnp.einsum(
        "qhd,khd->hqk", query_heads, key_heads, preferred_element_type=jnp.float32
    ) * (1.0 / math.sqrt(HD))
    scores = jnp.where(visible[None], scores, -1e30)
    row_top = jnp.max(scores, axis=2)
    weights = jnp.where(visible[None], jnp.exp(scores - row_top[:, :, None]), 0.0).astype(
        jnp.bfloat16
    )
    row_sum = jnp.sum(weights.astype(jnp.float32), axis=2)
    numerators = jnp.einsum(
        "hqk,khd->qhd", weights, value_heads, preferred_element_type=jnp.float32
    )
    return (row_top.T, row_sum.T, numerators)


def absorb(carry_state, request, partial_value):
    numer_all, top_all, sum_all = carry_state
    part_top, part_sum, part_numer = partial_value
    old_top = lax.dynamic_index_in_dim(top_all, request, 0, keepdims=False)
    old_sum = lax.dynamic_index_in_dim(sum_all, request, 0, keepdims=False)
    old_numer = lax.dynamic_index_in_dim(numer_all, request, 0, keepdims=False)
    new_top = jnp.maximum(old_top, part_top)
    old_factor = jnp.exp(old_top - new_top)
    part_factor = jnp.exp(part_top - new_top)
    merged_sum = old_factor * old_sum + part_factor * part_sum
    merged_numer = old_numer * old_factor[:, :, None] + part_numer * part_factor[:, :, None]
    return (
        lax.dynamic_update_index_in_dim(numer_all, merged_numer, request, 0),
        lax.dynamic_update_index_in_dim(top_all, new_top, request, 0),
        lax.dynamic_update_index_in_dim(sum_all, merged_sum, request, 0),
    )


def shards(
    queries,
    new_keys,
    new_values,
    key_cache,
    value_cache,
    out_weight,
    cache_len,
    page_table,
    block_perm,
):
    row_width = queries.shape[1]
    head_count = row_width // HD
    blk_count = lax.axis_size("blk")
    my_index = lax.axis_index("blk")
    req_count = cache_len.shape[0]
    blocks_per_req = NEW // TOK_DEV
    gathered = lax.all_gather(queries, "blk", axis=0, tiled=True)
    block_ids = jnp.arange(blk_count, dtype=jnp.int32)
    inverse = jnp.zeros((blk_count,), jnp.int32).at[block_perm].set(block_ids)
    query_all = gathered.reshape(blk_count, TOK_DEV, row_width)[inverse].reshape(
        req_count, NEW, row_width
    )
    global_ids = my_index * P_DEV + jnp.arange(P_DEV, dtype=jnp.int32)
    table_ids = jnp.arange(page_table.shape[0], dtype=jnp.int32)
    match_rows = page_table[None, :] == global_ids[:, None]
    logical = jnp.sum(jnp.where(match_rows, table_ids[None, :], 0), axis=1)
    page_req = logical // MAXP
    page_pos = logical % MAXP
    page_fill = jnp.clip(cache_len[page_req] - page_pos * PAGE, 0, PAGE)
    slot_ids = jnp.arange(PAGE, dtype=jnp.int32)
    start_state = (
        jnp.zeros((req_count, NEW, head_count, HD), jnp.float32),
        jnp.full((req_count, NEW, head_count), -1e30, jnp.float32),
        jnp.zeros((req_count, NEW, head_count), jnp.float32),
    )

    def page_work(slot_index, carry_state):
        request = page_req[slot_index]
        query_rows = lax.dynamic_index_in_dim(query_all, request, 0, keepdims=False)
        key_rows = lax.dynamic_index_in_dim(key_cache, slot_index, 0, keepdims=False)
        value_rows = lax.dynamic_index_in_dim(value_cache, slot_index, 0, keepdims=False)
        visible = jnp.broadcast_to((slot_ids < page_fill[slot_index])[None, :], (NEW, PAGE))
        return absorb(
            carry_state, request, block_partial(query_rows, key_rows, value_rows, visible)
        )

    def page_step(slot_index, carry_state):
        return page_work(slot_index, carry_state)

    carry_state = lax.fori_loop(0, P_DEV, page_step, start_state)
    my_block = block_perm[my_index]
    my_request = my_block // blocks_per_req
    my_offset = my_block % blocks_per_req * TOK_DEV
    new_pos = jnp.arange(NEW, dtype=jnp.int32)[:, None]
    key_pos = my_offset + jnp.arange(TOK_DEV, dtype=jnp.int32)[None, :]
    own_rows = lax.dynamic_index_in_dim(query_all, my_request, 0, keepdims=False)
    carry_state = absorb(
        carry_state, my_request, block_partial(own_rows, new_keys, new_values, new_pos >= key_pos)
    )
    numer_all, top_all, sum_all = carry_state
    send_numer = numer_all.reshape(blk_count, TOK_DEV, row_width)[block_perm]
    send_top = top_all.reshape(blk_count, TOK_DEV, head_count)[block_perm]
    send_sum = sum_all.reshape(blk_count, TOK_DEV, head_count)[block_perm]
    recv_numer, recv_top, recv_sum = (
        lax.all_to_all(send_numer, "blk", split_axis=0, concat_axis=0, tiled=True),
        lax.all_to_all(send_top, "blk", split_axis=0, concat_axis=0, tiled=True),
        lax.all_to_all(send_sum, "blk", split_axis=0, concat_axis=0, tiled=True),
    )
    best_top = jnp.max(recv_top, axis=0)
    factor = jnp.exp(recv_top - best_top[None])
    total_sum = jnp.sum(recv_sum * factor, axis=0)
    total_numer = jnp.sum(
        recv_numer.reshape(blk_count, TOK_DEV, head_count, HD) * factor[..., None], axis=0
    )
    mixed = (total_numer / total_sum[:, :, None]).reshape(TOK_DEV, row_width).astype(jnp.bfloat16)
    head_term = jnp.dot(mixed, out_weight, preferred_element_type=jnp.float32)
    return lax.psum_scatter(head_term, "head", scatter_dimension=1, tiled=True).astype(jnp.bfloat16)


def solution(mesh):
    in_specs = (
        P("blk", "head"),
        P("blk", "head"),
        P("blk", "head"),
        P("blk", None, "head"),
        P("blk", None, "head"),
        P("head", None),
        P(),
        P(),
        P(),
    )
    out_specs = P("blk", "head")
    return jax.shard_map(shards, mesh=mesh, in_specs=in_specs, out_specs=out_specs, check_vma=False)
```

profile of v0, /device:TPU:0, one launch (start us, length us, event | category | flops | bytes accessed | tf_op | source)
XLA Modules:
  0.0 454.9 jit_solution(13502735334571443504)
XLA Ops:
  10.8 1.3 reshape.103
  14.5 45.4 %all-gather.2.cloned.1.call-done = bf16[1024,1792]{1,0:T(8,128)(2,1)} async-done(((bf16[64,1792]{1,0:T(8,128)(2,1)}), bf16[1024,1792]{1,0:T(8,128)(2,1)}) %all-gather.2.cloned.1.call-update) | async-done | bytes 3670032 | tf_op jit(solution)/shard_map/all_gather | solution.py:71
  59.9 4.7 %gather_fusion = bf16[16,64,1792]{2,1,0:T(8,128)(2,1)} fusion(bf16[16,64,1792]{2,1,0:T(8,128)(2,1)} %bitcast.166, s32[1024]{0:T(1024)S(1)} %pad_clamp_fusion.1), kind=kCustom, calls=%fused_computation | custom fusion | bytes 7340096 | tf_op jit(solution)/shard_map/gather | solution.py:74
  64.5 9.3 %reshape.102 = bf16[1024,8,224]{2,1,0:T(8,128)(2,1)} reshape(bf16[16,64,1792]{2,1,0:T(8,128)(2,1)} %gather_fusion) | data formatting | bytes 7340032 | tf_op jit(solution)/shard_map/reshape | solution.py:18
  73.8 6.0 %copy.49 = bf16[1,1024,1792]{1,2,0:T(8,128)(2,1)} copy(bf16[1,1024,1792]{2,1,0:T(8,128)(2,1)} %bitcast.163) | data formatting | bytes 7340032
  79.8 3.9 broadcast_in_dim.148
  83.7 109.1 %while.18 = (s32[]{:T(128)}, f32[1,1024,8,224]{1,3,2,0:T(8,128)}, f32[1,1024,8]{1,2,0:T(8,128)S(1)}, f32[1,1024,8]{1,2,0:T(8,128)S(1)}, s32[8]{0:T(128)S(1)}, /*...) while((s32[]{:T(128)}, f32[1,1024,8,224]{1,3,2,0:T(8,128)}, ...), condition=%wide.region_5.6_spmd.clone, body=%wide.region_2.5_spmd.clone.sunk | while | flops 955547776 | bytes 87327304 | solution.py:104
  86.7 3.4 bitcast_reduce_fusion.3
  91.5 2.8 fusion.49
  94.4 3.0 copy-done
  100.4 3.4 bitcast_reduce_fusion.3
  105.2 2.8 fusion.49
  108.0 3.0 copy-done
  114.0 3.4 bitcast_reduce_fusion.3
  117.4 1.3 convert_reduce_fusion.3
  118.8 2.8 fusion.49
  121.6 3.0 copy-done
  127.6 3.4 bitcast_reduce_fusion.3
  132.4 2.8 fusion.49
  135.3 3.0 copy-done
  141.3 3.4 bitcast_reduce_fusion.3
  146.1 2.8 fusion.49
  148.9 3.0 copy-done
  154.9 3.4 bitcast_reduce_fusion.3
  159.7 2.8 fusion.49
  162.5 3.0 copy-done
  168.6 3.4 bitcast_reduce_fusion.3
  173.3 2.8 fusion.49
  176.2 3.0 copy-done
  182.2 3.4 bitcast_reduce_fusion.3
  187.0 2.8 fusion.49
  189.8 3.0 copy-done
  192.8 4.0 fusion.15
  198.8 3.7 all-to-all-start.2
  204.4 4.8 %all-to-all-done.2 = f32[16,1,512]{2,1,0:T(1,128)S(1)} async-done(((f32[16,1,512]{2,1,0:T(1,128)}), f32[16,1,512]{2,1,0:T(1,128)S(1)}, u32[]{:S(2)}, u32[]{:S(2)}) %all-to-all-start.2) | async-done | bytes 32800 | tf_op jit(solution)/shard_map/all_to_all | solution.py:121
  209.2 3.7 all-to-all-start.1
  212.9 7.6 %fusion.12 = f32[1024,8,224]{0,2,1:T(8,128)} fusion(f32[1,1024,8,224]{1,3,2,0:T(8,128)} %get-tuple-element.172, f32[1024,8]{0,1:T(8,128)S(1)} %get-tuple-element.258, f32[1024,8]{0,1:T(8,128)S(1)} %get-tuple-element.257, bf16[64,8,224]{2,1,0:T(8,128)(2,1)S(1)} %reshape.104, f32[8,1024,64]{1,2,0:T(8,128)S(1)} %get-tuple-element.266, ...), kind=kOutput, calls=%fused_computation.31 | convolution fusion | flops 243007488 | bytes 17170432 | tf_op jit(solution)/shard_map/hqk,khd->qhd/dot_general | solution.py:30
  220.5 9.2 %copy.54 = f32[1024,8,224]{2,1,0:T(8,128)} copy(f32[1024,8,224]{0,2,1:T(8,128)} %fusion.12) | data formatting | bytes 14680064 | tf_op jit(solution)/shard_map/add | solution.py:46
  229.7 10.5 %reshape.105 = f32[16,64,1792]{2,1,0:T(8,128)} reshape(f32[1024,8,224]{2,1,0:T(8,128)} %copy.54) | data formatting | bytes 14680064 | tf_op jit(solution)/shard_map/reshape | solution.py:115
  240.1 7.1 %gather_fusion.1 = f32[16,64,1792]{2,1,0:T(8,128)} fusion(f32[16,64,1792]{2,1,0:T(8,128)} %reshape.105, s32[1024]{0:T(1024)S(1)} %pad_clamp_fusion), kind=kCustom, calls=%fused_computation.1 | custom fusion | bytes 14680128 | tf_op jit(solution)/shard_map/gather | solution.py:115
  247.2 6.0 %all-to-all-start = ((f32[16,64,1792]{2,1,0:T(8,128)}), f32[16,64,1792]{2,1,0:T(8,128)}, u32[]{:S(2)}, u32[]{:S(2)}) async-start(f32[16,64,1792]{2,1,0:T(8,128)} %gather_fusion.1), calls=%async_computation | async-start | bytes 14680064 | tf_op jit(solution)/shard_map/all_to_all | solution.py:119
  256.2 3.8 mul.122
  260.0 10.5 %mul.123 = f32[16,64,1792]{2,1,0:T(8,128)} reshape(f32[16,64,8,224]{3,2,1,0:T(8,128)} %mul.122) | data formatting | bytes 14680064 | tf_op jit(solution)/shard_map/mul | solution.py:127
  270.6 115.2 %all-to-all-done = f32[16,64,1792]{2,1,0:T(8,128)} async-done(((f32[16,64,1792]{2,1,0:T(8,128)}), f32[16,64,1792]{2,1,0:T(8,128)}, u32[]{:S(2)}, u32[]{:S(2)}) %all-to-all-start) | async-done | bytes 7340064 | tf_op jit(solution)/shard_map/all_to_all | solution.py:119
  385.7 6.0 %multiply_reduce_fusion = f32[64,1792]{1,0:T(8,128)S(1)} fusion(f32[16,64,1792]{2,1,0:T(8,128)} %all-to-all-done, f32[16,64,1792]{2,1,0:T(8,128)} %mul.123), kind=kLoop, calls=%fused_computation.33 | loop fusion | flops 3555328 | bytes 15138816 | tf_op jit(solution)/shard_map/reduce_sum | solution.py:126
  391.8 7.9 %fusion.18 = f32[64,3584]{1,0:T(8,128)} fusion(bf16[1792,3584]{1,0:T(8,128)(2,1)} %param.16, f32[64,1792]{1,0:T(8,128)S(1)} %multiply_reduce_fusion, f32[64,1792]{1,0:T(8,128)S(1)} %div.18), kind=kOutput, calls=%fused_computation.44 | convolution fusion | flops 822312960 | bytes 14680064 | tf_op jit(solution)/shard_map/dot_general | solution.py:130
  399.7 46.6 %reduce-scatter.2.cloned.1.call-done = f32[64,1792]{1,0:T(8,128)} async-done(((f32[64,3584]{1,0:T(8,128)}), f32[64,1792]{1,0:T(8,128)}) %reduce-scatter.2.cloned.1.call-update) | async-done | bytes 458768 | tf_op jit(solution)/shard_map/reduce_scatter | solution.py:131
  446.3 1.7 convert_element_type.29
  (146 shorter events, 44.5 us)
Async XLA Ops:
  6.5 53.3 %all-gather.2.cloned.1.call-start = ((), (), s32[]{:S(2)}) async-start(), calls=%async_computation.4 | async-start | bytes 3899392 | tf_op jit(solution)/shard_map/all_gather | solution.py:71
  86.7 4.8 %slice-start = ((s8[7340032]{0:T(1024)(128)(4,1)}), s8[4194304]{0:T(1024)(128)(4,1)S(1)}, s32[]{:S(2)}) async-start(s8[7340032]{0:T(1024)(128)(4,1)} %bitcast.158), calls=%async_computation.6 | async-start | bytes 8388608 | tf_op jit(solution)/shard_map/while
  86.7 4.8 %slice-start.1 = ((s8[7340032]{0:T(1024)(128)(4,1)}), s8[3145728]{0:T(1024)(128)(4,1)S(1)}, s32[]{:S(2)}) async-start(s8[7340032]{0:T(1024)(128)(4,1)} %bitcast.158), calls=%async_computation.7 | async-start | bytes 6291456 | tf_op jit(solution)/shard_map/while
  94.3 3.0 copy-start
  100.4 4.8 %slice-start = ((s8[7340032]{0:T(1024)(128)(4,1)}), s8[4194304]{0:T(1024)(128)(4,1)S(1)}, s32[]{:S(2)}) async-start(s8[7340032]{0:T(1024)(128)(4,1)} %bitcast.158), calls=%async_computation.6 | async-start | bytes 8388608 | tf_op jit(solution)/shard_map/while
  100.4 4.8 %slice-start.1 = ((s8[7340032]{0:T(1024)(128)(4,1)}), s8[3145728]{0:T(1024)(128)(4,1)S(1)}, s32[]{:S(2)}) async-start(s8[7340032]{0:T(1024)(128)(4,1)} %bitcast.158), calls=%async_computation.7 | async-start | bytes 6291456 | tf_op jit(solution)/shard_map/while
  108.0 3.0 copy-start
  114.0 4.8 %slice-start = ((s8[7340032]{0:T(1024)(128)(4,1)}), s8[4194304]{0:T(1024)(128)(4,1)S(1)}, s32[]{:S(2)}) async-start(s8[7340032]{0:T(1024)(128)(4,1)} %bitcast.158), calls=%async_computation.6 | async-start | bytes 8388608 | tf_op jit(solution)/shard_map/while
  114.0 4.8 %slice-start.1 = ((s8[7340032]{0:T(1024)(128)(4,1)}), s8[3145728]{0:T(1024)(128)(4,1)S(1)}, s32[]{:S(2)}) async-start(s8[7340032]{0:T(1024)(128)(4,1)} %bitcast.158), calls=%async_computation.7 | async-start | bytes 6291456 | tf_op jit(solution)/shard_map/while
  121.6 3.0 copy-start
  127.6 4.8 %slice-start = ((s8[7340032]{0:T(1024)(128)(4,1)}), s8[4194304]{0:T(1024)(128)(4,1)S(1)}, s32[]{:S(2)}) async-start(s8[7340032]{0:T(1024)(128)(4,1)} %bitcast.158), calls=%async_computation.6 | async-start | bytes 8388608 | tf_op jit(solution)/shard_map/while
  127.6 4.8 %slice-start.1 = ((s8[7340032]{0:T(1024)(128)(4,1)}), s8[3145728]{0:T(1024)(128)(4,1)S(1)}, s32[]{:S(2)}) async-start(s8[7340032]{0:T(1024)(128)(4,1)} %bitcast.158), calls=%async_computation.7 | async-start | bytes 6291456 | tf_op jit(solution)/shard_map/while
  135.3 3.0 copy-start
  141.3 4.8 %slice-start = ((s8[7340032]{0:T(1024)(128)(4,1)}), s8[4194304]{0:T(1024)(128)(4,1)S(1)}, s32[]{:S(2)}) async-start(s8[7340032]{0:T(1024)(128)(4,1)} %bitcast.158), calls=%async_computation.6 | async-start | bytes 8388608 | tf_op jit(solution)/shard_map/while
  141.3 4.8 %slice-start.1 = ((s8[7340032]{0:T(1024)(128)(4,1)}), s8[3145728]{0:T(1024)(128)(4,1)S(1)}, s32[]{:S(2)}) async-start(s8[7340032]{0:T(1024)(128)(4,1)} %bitcast.158), calls=%async_computation.7 | async-start | bytes 6291456 | tf_op jit(solution)/shard_map/while
  148.9 3.0 copy-start
  154.9 4.8 %slice-start = ((s8[7340032]{0:T(1024)(128)(4,1)}), s8[4194304]{0:T(1024)(128)(4,1)S(1)}, s32[]{:S(2)}) async-start(s8[7340032]{0:T(1024)(128)(4,1)} %bitcast.158), calls=%async_computation.6 | async-start | bytes 8388608 | tf_op jit(solution)/shard_map/while
  154.9 4.8 %slice-start.1 = ((s8[7340032]{0:T(1024)(128)(4,1)}), s8[3145728]{0:T(1024)(128)(4,1)S(1)}, s32[]{:S(2)}) async-start(s8[7340032]{0:T(1024)(128)(4,1)} %bitcast.158), calls=%async_computation.7 | async-start | bytes 6291456 | tf_op jit(solution)/shard_map/while
  162.5 3.0 copy-start
  168.5 4.8 %slice-start = ((s8[7340032]{0:T(1024)(128)(4,1)}), s8[4194304]{0:T(1024)(128)(4,1)S(1)}, s32[]{:S(2)}) async-start(s8[7340032]{0:T(1024)(128)(4,1)} %bitcast.158), calls=%async_computation.6 | async-start | bytes 8388608 | tf_op jit(solution)/shard_map/while
  168.6 4.8 %slice-start.1 = ((s8[7340032]{0:T(1024)(128)(4,1)}), s8[3145728]{0:T(1024)(128)(4,1)S(1)}, s32[]{:S(2)}) async-start(s8[7340032]{0:T(1024)(128)(4,1)} %bitcast.158), calls=%async_computation.7 | async-start | bytes 6291456 | tf_op jit(solution)/shard_map/while
  176.2 3.0 copy-start
  182.2 4.8 %slice-start = ((s8[7340032]{0:T(1024)(128)(4,1)}), s8[4194304]{0:T(1024)(128)(4,1)S(1)}, s32[]{:S(2)}) async-start(s8[7340032]{0:T(1024)(128)(4,1)} %bitcast.158), calls=%async_computation.6 | async-start | bytes 8388608 | tf_op jit(solution)/shard_map/while
  182.2 4.8 %slice-start.1 = ((s8[7340032]{0:T(1024)(128)(4,1)}), s8[3145728]{0:T(1024)(128)(4,1)S(1)}, s32[]{:S(2)}) async-start(s8[7340032]{0:T(1024)(128)(4,1)} %bitcast.158), calls=%async_computation.7 | async-start | bytes 6291456 | tf_op jit(solution)/shard_map/while
  189.8 3.0 copy-start
  192.8 9.8 %copy-start.1 = (bf16[64,1792]{1,0:T(8,128)(2,1)S(1)}, bf16[64,1792]{1,0:T(8,128)(2,1)}, u32[]{:S(2)}) copy-start(bf16[64,1792]{1,0:T(8,128)(2,1)} %param.13) | copy-start | bytes 688132
  198.8 10.4 %all-to-all-start.2 = ((f32[16,1,512]{2,1,0:T(1,128)}), f32[16,1,512]{2,1,0:T(1,128)S(1)}, u32[]{:S(2)}, u32[]{:S(2)}) async-start(f32[16,1,512]{2,1,0:T(1,128)} %reshape.160), calls=%async_computation.2 | async-start | bytes 65536 | tf_op jit(solution)/shard_map/all_to_all | solution.py:121
  209.2 38.1 %all-to-all-start.1 = ((f32[16,1,512]{2,1,0:T(1,128)}), f32[16,1,512]{2,1,0:T(1,128)S(1)}, u32[]{:S(2)}, u32[]{:S(2)}) async-start(f32[16,1,512]{2,1,0:T(1,128)} %reshape.158), calls=%async_computation.1 | async-start | bytes 65536 | tf_op jit(solution)/shard_map/all_to_all | solution.py:120
  247.2 138.5 %all-to-all-start = ((f32[16,64,1792]{2,1,0:T(8,128)}), f32[16,64,1792]{2,1,0:T(8,128)}, u32[]{:S(2)}, u32[]{:S(2)}) async-start(f32[16,64,1792]{2,1,0:T(8,128)} %gather_fusion.1), calls=%async_computation | async-start | bytes 14680064 | tf_op jit(solution)/shard_map/all_to_all | solution.py:119
  253.3 193.0 %reduce-scatter.2.cloned.1.call-start = ((), (), s32[]{:S(2)}) async-start(), calls=%async_computation.5 | async-start | bytes 1376256 | tf_op jit(solution)/shard_map/reduce_scatter | solution.py:131
Sparse Core Ops, SparseCore 0:
  9.6 50.1 all-gather.1
  399.8 46.4 reduce-scatter.1
where the time goes:
time: 457 us; the launch traced here: 455 us
  waiting for transfers between devices  213 us (47%)
  local copies, waits for them, and re-layouts  116 us (25%)
  matrix products  69.3 us (15%)
  other arithmetic  27.3 us (6%)
  between operations  16 us (4%)
  starting transfers between devices  13.5 us (3%)
    all_to_all x1, waiting for transfers between devices, shards(): lax.all_to_all(send_numer, 'blk', split_axis=0, concat_axis=0, tiled=True)  115 us
    reduce_scatter x1, waiting for transfers between devices, shards(): lax.psum_scatter(head_term, 'head', scatter_dimension=1, tiled=True)  46.6 us
    all_gather x1, waiting for transfers between devices, shards(): gathered = lax.all_gather(queries, 'blk', axis=0, tiled=True)  45.4 us
    dot_general x9, matrix products, block_partial(): jnp.einsum('qhd,khd->hqk', query_heads, key_heads, preferred_element_type...  31.3 us
    dot_general x9, matrix products, block_partial(): jnp.einsum('hqk,khd->qhd', weights, value_heads, preferred_element_type=j...  30.1 us
    while x48, local copies, waits for them, and re-layouts  23.8 us
    mul x2, local copies, waits for them, and re-layouts, shards(): recv_numer.reshape(blk_count, TOK_DEV, head_count, HD) * factor[..., None]  14.4 us
    dynamic_slice x16, local copies, waits for them, and re-layouts, page_work(): lax.dynamic_index_in_dim(value_cache, slot_index, 0, keepdims=False)  11.9 us
  transfers between devices with their start and end apart: 5, of which 4 were waited for; matrix products, arithmetic and copies ran while one was open for 13% of the time, Pallas kernels for 0%

commit v1 on v0

--- a/solution.py
+++ b/solution.py
@@ -3,6 +3,8 @@
 import jax
 import jax.numpy as jnp
 from jax import lax
+from jax.experimental import pallas as pl
+from jax.experimental.pallas import tpu as pltpu
 from jax.sharding import PartitionSpec as P
 
 HD = 224
@@ -131,6 +133,321 @@
     return lax.psum_scatter(head_term, "head", scatter_dimension=1, tiled=True).astype(jnp.bfloat16)
 
 
+MESH = pl.DeviceIdType.MESH
+Z, Y, CORES, XS = 4, 2, 2, 2
+HEADS_CORE = 4
+GROUP = HEADS_CORE * HD
+CACHED = CORES * P_DEV * PAGE
+FRESH = CORES * TOK_DEV
+KEYS = CACHED + FRESH
+QCHIP = CORES * TOK_DEV
+QW = Y * QCHIP
+VROWS = HD + 16
+COLS = 1792
+LOG2_SCALE = math.log2(math.e) / math.sqrt(HD)
+
+
+def fits_fused(mesh):
+    return dict(mesh.shape) == {"blk": Z * Y * CORES, "head": XS}
+
+
+def fused_kernel(
+    perm, q_hbm, nk_hbm, nv_hbm, kc_hbm, vc_hbm, w_hbm, out_ref,
+    q_stage, nk_stage, nv_stage, k_stage, v_stage, w_all,
+    q_t, k_heads, v_t, scores, probs,
+    part, part_16, part_stat, y_part, y_stat,
+    z_src, z_src_stat, z_part, z_stat,
+    acc, c_part, x_src, x_part,
+    local_sem, core_send, core_recv, gz_send, gz_recv, gy_send, gy_recv,
+    ry_send, ry_recv, rz_send, rz_recv, o_send, o_recv,
+):
+    me = lax.axis_index("blk")
+    x = lax.axis_index("head")
+    core = me % CORES
+    y = (me // CORES) % Y
+    z = me // (CORES * Y)
+
+    def blk_of(zz, yy, cc):
+        return (zz * Y + yy) * CORES + cc
+
+    sibling = (blk_of(z, y, 1 - core), x)
+    y_peer = (blk_of(z, 1 - y, core), x)
+    x_peer = (me, 1 - x)
+    z_to = [None] + [(blk_of((z + d) % Z, y, core), x) for d in range(1, Z)]
+    barrier = pltpu.get_barrier_semaphore()
+    for peer in [sibling, y_peer, x_peer] + z_to[1:]:
+        pl.semaphore_signal(barrier, inc=1, device_id=peer, device_id_type=MESH)
+    pl.semaphore_wait(barrier, Z + 2)
+
+    mine = pl.ds(pl.multiple_of(core * GROUP, 128), GROUP)
+    theirs = pl.ds(pl.multiple_of((1 - core) * GROUP, 128), GROUP)
+    staged = [
+        (q_hbm, q_stage), (kc_hbm, k_stage), (vc_hbm, v_stage),
+        (nk_hbm, nk_stage), (nv_hbm, nv_stage),
+    ]
+    local_copies, core_copies = [], []
+    for i, (src, dst) in enumerate(staged):
+        lead = (slice(None),) * (len(src.shape) - 1)
+        copy = pltpu.make_async_copy(src.at[lead + (mine,)], dst.at[core], local_sem.at[i])
+        copy.start()
+        local_copies.append(copy)
+        copy = pltpu.make_async_remote_copy(
+            src_ref=src.at[lead + (theirs,)], dst_ref=dst.at[core],
+            send_sem=core_send.at[i], recv_sem=core_recv.at[i],
+            device_id=sibling, device_id_type=MESH)
+        copy.start()
+        core_copies.append(copy)
+    w_copy = pltpu.make_async_copy(
+        w_hbm.at[pl.ds(pl.multiple_of(core * GROUP, 128), GROUP), :], w_all, local_sem.at[5])
+    w_copy.start()
+
+    pending = list(core_copies)
+
+    def remote(src, dst, send_sem, recv_sem, peer):
+        copy = pltpu.make_async_remote_copy(
+            src_ref=src, dst_ref=dst, send_sem=send_sem, recv_sem=recv_sem,
+            device_id=peer, device_id_type=MESH)
+        copy.start()
+        return copy
+
+    local_copies[0].wait()
+    core_copies[0].wait_recv()
+    q_rows = jnp.concatenate([q_stage[0], q_stage[1]], axis=0).astype(jnp.float32)
+    q_cols = q_rows.T.astype(jnp.bfloat16)
+    for h in range(HEADS_CORE):
+        q_t[h, z, y] = q_cols[h * HD:(h + 1) * HD]
+
+    gather_z, gather_y, red_y, red_z = {}, {}, {}, {}
+    for h in range(HEADS_CORE):
+        block = q_t.at[h, z, y]
+        gather_y[h, 0] = remote(block, block, gy_send.at[h, 0], gy_recv.at[h, 0], y_peer)
+        for d in range(1, Z):
+            gather_z[h, d] = remote(block, block, gz_send.at[h, d], gz_recv.at[h, d], z_to[d])
+
+    def forward(h):
+        for d in range(1, Z):
+            gather_z[h, d].wait_recv()
+            block = q_t.at[h, (z + Z - d) % Z, y]
+            gather_y[h, d] = remote(block, block, gy_send.at[h, d], gy_recv.at[h, d], y_peer)
+
+    def place_keys(rows, at, count):
+        wide = rows.astype(jnp.float32)
+        for h in range(HEADS_CORE):
+            k_heads[h, pl.ds(at, count), :] = wide[:, h * HD:(h + 1) * HD].astype(jnp.bfloat16)
+
+    def place_values(rows, at):
+        tall = rows.astype(jnp.float32).T.astype(jnp.bfloat16)
+        for h in range(HEADS_CORE):
+            v_t[h, pl.ds(0, HD), pl.ds(at, PAGE)] = tall[h * HD:(h + 1) * HD]
+
+    v_t[:, pl.ds(HD, VROWS - HD), :] = jnp.ones((HEADS_CORE, VROWS - HD, KEYS), jnp.bfloat16)
+
+    local_copies[1].wait()
+    core_copies[1].wait_recv()
+
+    @pl.loop(0, CORES * P_DEV)
+    def _(page):
+        at = pl.multiple_of(page * PAGE, PAGE)
+        place_keys(k_stage[page // P_DEV, page % P_DEV], at, PAGE)
+
+    forward(0)
+    local_copies[2].wait()
+    core_copies[2].wait_recv()
+
+    @pl.loop(0, CORES * P_DEV)
+    def _(page):
+        at = pl.multiple_of(page * PAGE, PAGE)
+        place_values(v_stage[page // P_DEV, page % P_DEV], at)
+
+    local_copies[3].wait()
+    core_copies[3].wait_recv()
+    local_copies[4].wait()
+    core_copies[4].wait_recv()
+    place_keys(jnp.concatenate([nk_stage[0], nk_stage[1]], axis=0), CACHED, FRESH)
+    place_values(jnp.concatenate([nv_stage[0], nv_stage[1]], axis=0), CACHED)
+
+    row = lax.broadcasted_iota(jnp.int32, (FRESH, QW), 0)
+    lane = lax.broadcasted_iota(jnp.int32, (FRESH, QW), 1)
+    key_pos = jnp.where(
+        row < TOK_DEV, perm[blk_of(z, y, 0)], perm[blk_of(z, y, 1)]) * TOK_DEV + row % TOK_DEV
+    tile_row = lax.broadcasted_iota(jnp.int32, (8, QCHIP), 0)
+
+    def attend(h):
+        @pl.loop(0, Z)
+        def _(g):
+            queries = jnp.concatenate([q_t[h, g, 0], q_t[h, g, 1]], axis=1)
+            query_blk = jnp.zeros((FRESH, QW), jnp.int32)
+            for j in range(Y * CORES):
+                query_blk = jnp.where(lane // TOK_DEV == j, perm[g * Y * CORES + j], query_blk)
+            seen = query_blk * TOK_DEV + lane % TOK_DEV >= key_pos
+            fresh = jnp.dot(
+                k_heads[h, pl.ds(CACHED, FRESH), :], queries, preferred_element_type=jnp.float32)
+            fresh = jnp.where(seen, fresh, -1e30)
+            scores[pl.ds(CACHED, FRESH), :] = fresh
+            top = jnp.max(fresh.reshape(FRESH // 8, 8, QW), axis=0)
+            for i in range(CACHED // 256):
+                tile = jnp.dot(
+                    k_heads[h, pl.ds(i * 256, 256), :], queries,
+                    preferred_element_type=jnp.float32)
+                scores[pl.ds(i * 256, 256), :] = tile
+                top = jnp.maximum(top, jnp.max(tile.reshape(32, 8, QW), axis=0))
+            top = jnp.max(top, axis=0, keepdims=True) * LOG2_SCALE
+            for i in range(KEYS // 128):
+                tile = scores[pl.ds(i * 128, 128), :]
+                probs[pl.ds(i * 128, 128), :] = jnp.exp2(tile * LOG2_SCALE - top).astype(
+                    jnp.bfloat16)
+            numer = jnp.dot(v_t[h], probs[...], preferred_element_type=jnp.float32)
+            for j in range(Y):
+                cols = slice(j * QCHIP, (j + 1) * QCHIP)
+                part[h, j, g] = numer[:HD, cols]
+                part_16[h, j, g] = numer[:HD, cols].astype(jnp.bfloat16)
+                part_stat[h, j, g] = jnp.where(
+                    tile_row == 0, top[:, cols], numer[HD:HD + 1, cols])
+
+    def send_y(h):
+        red_y[h] = (
+            remote(part_16.at[h, 1 - y], y_part.at[h], ry_send.at[h, 0], ry_recv.at[h, 0], y_peer),
+            remote(part_stat.at[h, 1 - y], y_stat.at[h], ry_send.at[h, 1], ry_recv.at[h, 1], y_peer),
+        )
+
+    def merge_y(h):
+        for copy in red_y[h]:
+            copy.wait_recv()
+
+        @pl.loop(0, Z)
+        def _(g):
+            own, other = part_stat[h, y, g], y_stat[h, g]
+            top = jnp.maximum(own[0:1], other[0:1])
+            own_factor, other_factor = jnp.exp2(own[0:1] - top), jnp.exp2(other[0:1] - top)
+            total = own[1:2] * own_factor + other[1:2] * other_factor
+            numer = part[h, y, g] * own_factor + y_part[h, g].astype(jnp.float32) * other_factor
+            z_src[h, g] = numer.astype(jnp.bfloat16)
+            z_src_stat[h, g] = jnp.where(tile_row == 0, top, total)
+
+        for d in range(1, Z):
+            to = (z + d) % Z
+            red_z[h, d] = (
+                remote(z_src.at[h, to], z_part.at[h, d], rz_send.at[h, d, 0], rz_recv.at[h, d, 0], z_to[d]),
+                remote(z_src_stat.at[h, to], z_stat.at[h, d], rz_send.at[h, d, 1], rz_recv.at[h, d, 1], z_to[d]),
+            )
+
+    def finish(h):
+        for d in range(1, Z):
+            for copy in red_z[h, d]:
+                copy.wait_recv()
+        stats = [z_src_stat[h, z]] + [z_stat[h, d] for d in range(1, Z)]
+        numers = [z_src[h, z]] + [z_part[h, d] for d in range(1, Z)]
+        top = stats[0][0:1]
+        for stat in stats[1:]:
+            top = jnp.maximum(top, stat[0:1])
+        total = jnp.zeros((1, QCHIP), jnp.float32)
+        numer = jnp.zeros((HD, QCHIP), jnp.float32)
+        for stat, term in zip(stats, numers):
+            factor = jnp.exp2(stat[0:1] - top)
+            total = total + stat[1:2] * factor
+            numer = numer + term.astype(jnp.float32) * factor
+        mixed = (numer / total).T.astype(jnp.bfloat16)
+        for half in range(XS):
+            for i in range(COLS // 256):
+                cols = pl.ds(i * 256, 256)
+                term = jnp.dot(
+                    mixed, w_all[pl.ds(h * HD, HD), pl.ds(half * COLS + i * 256, 256)],
+                    preferred_element_type=jnp.float32)
+                for c in range(CORES):
+                    rows = term[c * TOK_DEV:(c + 1) * TOK_DEV]
+                    if h == 0:
+                        acc[half, c, :, cols] = rows
+                    else:
+                        acc[half, c, :, cols] += rows
+
+    for h in range(HEADS_CORE):
+        if h + 1 < HEADS_CORE:
+            forward(h + 1)
+        for d in range(Z):
+            gather_y[h, d].wait_recv()
+        attend(h)
+        send_y(h)
+        if h == 0:
+            w_copy.wait()
+        if h >= 1:
+            merge_y(h - 1)
+        if h >= 2:
+            finish(h - 2)
+    merge_y(HEADS_CORE - 1)
+    finish(HEADS_CORE - 2)
+    finish(HEADS_CORE - 1)
+
+    away = remote(acc.at[1 - x, 1 - core], c_part.at[0], o_send.at[0], o_recv.at[0], sibling)
+    home = remote(acc.at[x, 1 - core], c_part.at[1], o_send.at[1], o_recv.at[1], sibling)
+    away.wait_recv()
+    x_src[...] = (acc[1 - x, core] + c_part[0]).astype(jnp.bfloat16)
+    across = remote(x_src, x_part, o_send.at[2], o_recv.at[2], x_peer)
+    home.wait_recv()
+    c_part[1] = acc[x, core] + c_part[1]
+    across.wait_recv()
+    out_ref[...] = (c_part[1] + x_part[...].astype(jnp.float32)).astype(jnp.bfloat16)
+
+    pending += [away, home, across]
+    pending += list(gather_z.values()) + list(gather_y.values())
+    for copies in list(red_y.values()) + list(red_z.values()):
+        pending += list(copies)
+    for copy in pending:
+        copy.wait_send()
+
+
+def fused_shards(
+    queries, new_keys, new_values, key_cache, value_cache, out_weight,
+    cache_len, page_table, block_perm,
+):
+    bf16, f32 = jnp.bfloat16, jnp.float32
+    vmem, dma = pltpu.VMEM, pltpu.SemaphoreType.DMA
+    hc = HEADS_CORE
+    block = (HD, QCHIP)
+    stat = (8, QCHIP)
+    scratch = [
+        vmem((CORES, TOK_DEV, GROUP), bf16),
+        vmem((CORES, TOK_DEV, GROUP), bf16),
+        vmem((CORES, TOK_DEV, GROUP), bf16),
+        vmem((CORES, P_DEV, PAGE, GROUP), bf16),
+        vmem((CORES, P_DEV, PAGE, GROUP), bf16),
+        vmem((GROUP, XS * COLS), bf16),
+        vmem((hc, Z, Y) + block, bf16),
+        vmem((hc, KEYS, HD), bf16),
+        vmem((hc, VROWS, KEYS), bf16),
+        vmem((KEYS, QW), f32),
+        vmem((KEYS, QW), bf16),
+        vmem((hc, Y, Z) + block, f32),
+        vmem((hc, Y, Z) + block, bf16),
+        vmem((hc, Y, Z) + stat, f32),
+        vmem((hc, Z) + block, bf16),
+        vmem((hc, Z) + stat, f32),
+        vmem((hc, Z) + block, bf16),
+        vmem((hc, Z) + stat, f32),
+        vmem((hc, Z) + block, bf16),
+        vmem((hc, Z) + stat, f32),
+        vmem((XS, CORES, TOK_DEV, COLS), f32),
+        vmem((2, TOK_DEV, COLS), f32),
+        vmem((TOK_DEV, COLS), bf16),
+        vmem((TOK_DEV, COLS), bf16),
+        dma((6,)), dma((5,)), dma((5,)),
+        dma((hc, Z)), dma((hc, Z)), dma((hc, Z)), dma((hc, Z)),
+        dma((hc, 2)), dma((hc, 2)), dma((hc, Z, 2)), dma((hc, Z, 2)),
+        dma((3,)), dma((3,)),
+    ]
+    flops = 4 * hc * Z * QW * KEYS * HD + 2 * QCHIP * GROUP * XS * COLS
+    return pl.pallas_call(
+        fused_kernel,
+        out_shape=jax.ShapeDtypeStruct((TOK_DEV, COLS), bf16),
+        in_specs=[pl.BlockSpec(memory_space=pltpu.SMEM)] + [pl.BlockSpec(memory_space=pl.ANY)] * 6,
+        out_specs=pl.BlockSpec(memory_space=pltpu.VMEM),
+        scratch_shapes=scratch,
+        compiler_params=pltpu.CompilerParams(
+            collective_id=0, has_side_effects=True, vmem_limit_bytes=56 * 1024 * 1024),
+        cost_estimate=pl.CostEstimate(
+            flops=flops, bytes_accessed=14 * 1024 * 1024, transcendentals=hc * Z * QW * KEYS),
+    )(block_perm, queries, new_keys, new_values, key_cache, value_cache, out_weight)
+
+
 def solution(mesh):
     in_specs = (
         P("blk", "head"),
@@ -144,4 +461,5 @@
         P(),
     )
     out_specs = P("blk", "head")
-    return jax.shard_map(shards, mesh=mesh, in_specs=in_specs, out_specs=out_specs, check_vma=False)
+    local = fused_shards if fits_fused(mesh) else shards
+    return jax.shard_map(local, mesh=mesh, in_specs=in_specs, out_specs=out_specs, check_vma=False)

time: 457 us -> 79.1 us (0.17)
  waiting for transfers between devices: 213 us -> 0 us
  local copies, waits for them, and re-layouts: 116 us -> 1.64 us
  Pallas kernels: 0 us -> 76.7 us
  matrix products: 69.3 us -> 0 us
  other arithmetic: 27.3 us -> 0 us
  between operations: 16 us -> 0.01 us
  starting transfers between devices: 13.5 us -> 0 us
    all_to_all x3 -> x0, waiting for transfers between devices: 120 us -> none  [the longest x1 115 us: shards(): lax.all_to_all(send_numer, 'blk', split_axis=0, concat_axis=0, tiled=True)]
    pallas_call x0 -> x1, Pallas kernels: none -> 76.7 us  [fused_shards(): pl.pallas_call(fused_kernel, out_shape=jax.ShapeDtypeStruct((TOK_DEV, COL...]
    dot_general x19 -> x0, matrix products: 69.3 us -> none  [the longest x9 31.3 us: block_partial(): jnp.einsum('qhd,khd->hqk', query_heads, key_heads, preferred_element_type...]
    reduce_scatter x1 -> x0, waiting for transfers between devices: 46.6 us -> none  [shards(): lax.psum_scatter(head_term, 'head', scatter_dimension=1, tiled=True)]
    all_gather x1 -> x0, waiting for transfers between devices: 45.4 us -> none  [shards(): gathered = lax.all_gather(queries, 'blk', axis=0, tiled=True)]
    while x48 -> x0, local copies, waits for them, and re-layouts: 23.8 us -> none
    reshape x8 -> x0, local copies, waits for them, and re-layouts: 21.7 us -> none  [the longest x1 10.5 us: shards(): send_numer = numer_all.reshape(blk_count, TOK_DEV, row_width)[block_perm]]
    dynamic_slice x33 -> x0, local copies, waits for them, and re-layouts: 20.3 us -> none  [the longest x16 11.9 us: page_work(): lax.dynamic_index_in_dim(value_cache, slot_index, 0, keepdims=False)]
  transfers between devices with their start and end apart: 5 -> 0, of which waited for: 4 -> 0; matrix products, arithmetic and copies ran while one was open for 13% -> 0% of each run, Pallas kernels for 0% -> 0%
where the time goes in v1:
time: 79.1 us; the launch traced here: 78.4 us
  Pallas kernels  76.7 us (97%)
  local copies, waits for them, and re-layouts  1.64 us (2%)
    pallas_call x1, Pallas kernels, fused_shards(): pl.pallas_call(fused_kernel, out_shape=jax.ShapeDtypeStruct((TOK_DEV, COL...  76.7 us
    unnamed x1, local copies, waits for them, and re-layouts  1.64 us

profile of v1, /device:TPU:0, one launch (start us, length us, event | category | flops | bytes accessed | tf_op | source)
XLA Modules:
  0.0 78.4 jit_solution(11771223938326708691)
XLA Ops:
  0.0 76.7 %shard_map.73 = bf16[64,1792]{1,0:T(8,128)(2,1)} custom-call(s32[16]{0:T(128)} %perm.1, bf16[64,1792]{1,0:T(8,128)(2,1)} %q_hbm.1, bf16[64,1792]{1,0:T(8,128)(2,1)} %nk_hbm.1, bf16[64,1792]{1,0:T(8,128)(2,1)} %nv_hbm.1, bf16[8,128,1792]{2,1,0:T(8,128)(2,1)} %kc_hbm.1, bf16[8,128,1792]{2,1,0:T(8,128)(2,1)} %vc_hbm.1, bf16[1792,3584]{1,0:T(8,128)(2,1)} %w_hbm.1), custom_call_target="tpu_custom_call" | custom-call | flops 8808038400 | bytes 14680064 | tf_op jit(solution)/shard_map/pallas_call | solution.py:438
  76.8 1.6 %copy.9 = bf16[64,1792]{1,0:T(8,128)(2,1)} copy(bf16[64,1792]{1,0:T(8,128)(2,1)} %shard_map.73) | data formatting | bytes 458752

commit v2 on v0

--- a/solution.py
+++ b/solution.py
@@ -3,6 +3,8 @@
 import jax
 import jax.numpy as jnp
 from jax import lax
+from jax.experimental import pallas as pl
+from jax.experimental.pallas import tpu as pltpu
 from jax.sharding import PartitionSpec as P
 
 HD = 224
@@ -131,6 +133,455 @@
     return lax.psum_scatter(head_term, "head", scatter_dimension=1, tiled=True).astype(jnp.bfloat16)
 
 
+MESH = pl.DeviceIdType.MESH
+Z, Y, CORES, XS = 4, 2, 2, 2
+HEADS_CORE = 4
+GROUP = HEADS_CORE * HD
+CACHED = CORES * P_DEV * PAGE
+FRESH = CORES * TOK_DEV
+KEYS = CACHED + FRESH
+QCHIP = CORES * TOK_DEV
+QW = Y * QCHIP
+VROWS = HD + 16
+COLS = 1792
+CHUNK = COLS // 2
+WINDOW = 384
+UNITS = HEADS_CORE * Z
+LAG = 2
+LOG2_SCALE = math.log2(math.e) / math.sqrt(HD)
+
+
+def fits_fused(mesh):
+    return dict(mesh.shape) == {"blk": Z * Y * CORES, "head": XS}
+
+
+def fused_kernel(
+    perm, q_hbm, nk_hbm, nv_hbm, kc_hbm, vc_hbm, w_hbm, out_ref,
+    q_stage, nk_stage, nv_stage, k_stage, v_stage, w_all,
+    q_t, k_heads, v_t, scores_a, scores_b, probs_a, probs_b, tops,
+    part, part_16, part_stat, y_part, y_stat,
+    z_src, z_src_stat, z_part, z_stat,
+    acc, c_part, x_src, x_part,
+    local_sem, core_send, core_recv, gz_send, gz_recv, gy_send, gy_recv,
+    ry_send, ry_recv, rz_send, rz_recv, o_send, o_recv,
+):
+    me = lax.axis_index("blk")
+    x = lax.axis_index("head")
+    core = me % CORES
+    y = (me // CORES) % Y
+    z = me // (CORES * Y)
+    scores, probs = (scores_a, scores_b), (probs_a, probs_b)
+
+    def blk_of(zz, yy, cc):
+        return (zz * Y + yy) * CORES + cc
+
+    sibling = (blk_of(z, y, 1 - core), x)
+    y_peer = (blk_of(z, 1 - y, core), x)
+    x_peer = (me, 1 - x)
+
+    def z_to(d):
+        return (blk_of((z + d) % Z, y, core), x)
+
+    barrier = pltpu.get_barrier_semaphore()
+    for peer in [sibling, y_peer, x_peer] + [z_to(d) for d in range(1, Z)]:
+        pl.semaphore_signal(barrier, inc=1, device_id=peer, device_id_type=MESH)
+    pl.semaphore_wait(barrier, Z + 2)
+
+    def remote(src, dst, send_sem, recv_sem, peer):
+        return pltpu.make_async_remote_copy(
+            src_ref=src, dst_ref=dst, send_sem=send_sem, recv_sem=recv_sem,
+            device_id=peer, device_id_type=MESH)
+
+    mine = pl.ds(pl.multiple_of(core * GROUP, 128), GROUP)
+    theirs = pl.ds(pl.multiple_of((1 - core) * GROUP, 128), GROUP)
+    staged = [
+        (q_hbm, q_stage), (kc_hbm, k_stage), (nk_hbm, nk_stage),
+        (vc_hbm, v_stage), (nv_hbm, nv_stage),
+    ]
+    local_copies, core_copies = [], []
+    for i, (src, dst) in enumerate(staged):
+        lead = (slice(None),) * (len(src.shape) - 1)
+        copy = remote(
+            src.at[lead + (theirs,)], dst.at[core], core_send.at[i], core_recv.at[i], sibling)
+        copy.start()
+        core_copies.append(copy)
+        copy = pltpu.make_async_copy(src.at[lead + (mine,)], dst.at[core], local_sem.at[i])
+        copy.start()
+        local_copies.append(copy)
+    w_copy = pltpu.make_async_copy(
+        w_hbm.at[pl.ds(pl.multiple_of(core * GROUP, 128), GROUP), :], w_all, local_sem.at[5])
+    w_copy.start()
+
+    def arrived(i):
+        local_copies[i].wait()
+        core_copies[i].wait_recv()
+
+    def gather_z(h, d):
+        block = q_t.at[h, z, y]
+        return remote(block, block, gz_send.at[h, d], gz_recv.at[h, d], z_to(d))
+
+    def gather_y(h, d):
+        block = q_t.at[h, (z + Z - d) % Z, y]
+        return remote(block, block, gy_send.at[h, d], gy_recv.at[h, d], y_peer)
+
+    def forward(h, d):
+        gather_z(h, d).wait_recv()
+        gather_y(h, d).start()
+
+    def reduce_y(h, g):
+        return (
+            remote(part_16.at[h, g, 1 - y], y_part.at[h, g],
+                   ry_send.at[h, g, 0], ry_recv.at[h, g, 0], y_peer),
+            remote(part_stat.at[h, g, 1 - y], y_stat.at[h, g],
+                   ry_send.at[h, g, 1], ry_recv.at[h, g, 1], y_peer),
+        )
+
+    def reduce_z(h, d):
+        to = (z + d) % Z
+        return (
+            remote(z_src.at[h, to], z_part.at[h, d],
+                   rz_send.at[h, d, 0], rz_recv.at[h, d, 0], z_to(d)),
+            remote(z_src_stat.at[h, to], z_stat.at[h, d],
+                   rz_send.at[h, d, 1], rz_recv.at[h, d, 1], z_to(d)),
+        )
+
+    arrived(0)
+    q_rows = jnp.concatenate([q_stage[0], q_stage[1]], axis=0).astype(jnp.float32)
+    q_cols = q_rows.T.astype(jnp.bfloat16)
+    for h in range(HEADS_CORE):
+        q_t[h, z, y] = q_cols[h * HD:(h + 1) * HD]
+    for h in range(HEADS_CORE):
+        gather_y(h, 0).start()
+        for d in range(1, Z):
+            gather_z(h, d).start()
+
+    v_t[:, pl.ds(HD, VROWS - HD), :] = jnp.ones((HEADS_CORE, VROWS - HD, KEYS), jnp.bfloat16)
+    acc[...] = jnp.zeros(acc.shape, jnp.float32)
+
+    def head_window(h):
+        start = jnp.minimum(h * HD // 128 * 128, GROUP - WINDOW)
+        return pl.ds(pl.multiple_of(start, 128), WINDOW), h * HD - start
+
+    def prepare_keys(h):
+        window, offset = head_window(h)
+        pick = jnp.where(
+            lax.broadcasted_iota(jnp.int32, (WINDOW, HD), 0)
+            == lax.broadcasted_iota(jnp.int32, (WINDOW, HD), 1) + offset, 1.0, 0.0
+        ).astype(jnp.bfloat16)
+
+        def place(rows, at, count):
+            k_heads[h, pl.ds(at, count), :] = jnp.dot(
+                rows, pick, preferred_element_type=jnp.float32).astype(jnp.bfloat16)
+
+        for c in range(CORES):
+            for page in range(0, P_DEV, 2):
+                rows = k_stage[c, pl.ds(page, 2), :, window].reshape(2 * PAGE, WINDOW)
+                place(rows, (c * P_DEV + page) * PAGE, 2 * PAGE)
+            place(nk_stage[c, :, window], CACHED + c * TOK_DEV, TOK_DEV)
+
+    def prepare_values(h):
+        window, offset = head_window(h)
+        pick = jnp.where(
+            lax.broadcasted_iota(jnp.int32, (HD, WINDOW), 1)
+            == lax.broadcasted_iota(jnp.int32, (HD, WINDOW), 0) + offset, 1.0, 0.0
+        ).astype(jnp.bfloat16)
+
+        def place(rows, at, count):
+            v_t[h, pl.ds(0, HD), pl.ds(at, count)] = lax.dot_general(
+                pick, rows, (((1,), (1,)), ((), ())), preferred_element_type=jnp.float32
+            ).astype(jnp.bfloat16)
+
+        for c in range(CORES):
+            for page in range(0, P_DEV, 2):
+                rows = v_stage[c, pl.ds(page, 2), :, window].reshape(2 * PAGE, WINDOW)
+                place(rows, (c * P_DEV + page) * PAGE, 2 * PAGE)
+        place(jnp.concatenate([nv_stage[c, :, window] for c in range(CORES)], axis=0), CACHED, FRESH)
+
+    row = lax.broadcasted_iota(jnp.int32, (FRESH, QW), 0)
+    lane = lax.broadcasted_iota(jnp.int32, (FRESH, QW), 1)
+    tile_row = lax.broadcasted_iota(jnp.int32, (8, QCHIP), 0)
+
+    def unit_of(u):
+        h, t = u // Z, u % Z
+        return h, (t + h // (HEADS_CORE - 1)) % Z
+
+    def score_tiles(u, par):
+        h, k = unit_of(u)
+        g = (z + k) % Z
+        queries = jnp.concatenate([q_t[h, g, 0], q_t[h, g, 1]], axis=1)
+        top = [None]
+
+        def cached(i):
+            tile = jnp.dot(
+                k_heads[h, pl.ds(i * 256, 256), :], queries, preferred_element_type=jnp.float32)
+            scores[par][pl.ds(i * 256, 256), :] = tile
+            tile_top = jnp.max(tile.reshape(32, 8, QW), axis=0)
+            top[0] = tile_top if top[0] is None else jnp.maximum(top[0], tile_top)
+
+        def fresh():
+            key_pos = jnp.where(
+                row < TOK_DEV, perm[blk_of(z, y, 0)], perm[blk_of(z, y, 1)]
+            ) * TOK_DEV + row % TOK_DEV
+            query_blk = jnp.zeros((FRESH, QW), jnp.int32)
+            for j in range(Y * CORES):
+                query_blk = jnp.where(lane // TOK_DEV == j, perm[g * Y * CORES + j], query_blk)
+            seen = query_blk * TOK_DEV + lane % TOK_DEV >= key_pos
+            tile = jnp.dot(
+                k_heads[h, pl.ds(CACHED, FRESH), :], queries, preferred_element_type=jnp.float32)
+            tile = jnp.where(seen, tile, -1e30)
+            scores[par][pl.ds(CACHED, FRESH), :] = tile
+            all_top = jnp.maximum(top[0], jnp.max(tile.reshape(FRESH // 8, 8, QW), axis=0))
+            tops[par] = jnp.broadcast_to(
+                jnp.max(all_top, axis=0, keepdims=True) * LOG2_SCALE, (8, QW))
+
+        return [lambda i=i: cached(i) for i in range(CACHED // 256)] + [fresh]
+
+    def weight_tiles(par):
+        top = tops[par][0:1]
+        tops[2 + par] = tops[par]
+
+        def weigh(at, count):
+            tile = scores[par][pl.ds(at, count), :]
+            probs[par][pl.ds(at, count), :] = jnp.exp2(tile * LOG2_SCALE - top).astype(jnp.bfloat16)
+
+        spans = [(i * 256, 256) for i in range(CACHED // 256)] + [(CACHED, FRESH)]
+        return [lambda s=s: weigh(*s) for s in spans]
+
+    def value_tiles(u, par, numer):
+        h, _ = unit_of(u)
+
+        def add(at, count):
+            term = jnp.dot(
+                v_t[h, :, pl.ds(at, count)], probs[par][pl.ds(at, count), :],
+                preferred_element_type=jnp.float32)
+            numer[0] = term if numer[0] is None else numer[0] + term
+
+        def nothing():
+            pass
+
+        steps = [nothing] * 9
+        for slot, at, count in ((0, 0, 768), (3, 768, 768), (6, 1536, 640)):
+            steps[slot] = lambda at=at, count=count: add(at, count)
+        return steps
+
+    def merge(u):
+        h, k = unit_of(u)
+        g = (z + k) % Z
+        for copy in reduce_y(h, g):
+            copy.wait_recv()
+        own, other = part_stat[h, g, y], y_stat[h, g]
+        top = jnp.maximum(own[0:1], other[0:1])
+        own_factor, other_factor = jnp.exp2(own[0:1] - top), jnp.exp2(other[0:1] - top)
+        total = own[1:2] * own_factor + other[1:2] * other_factor
+        numer = part[h, g, y] * own_factor + y_part[h, g].astype(jnp.float32) * other_factor
+        z_src[h, g] = numer.astype(jnp.bfloat16)
+        z_src_stat[h, g] = jnp.where(tile_row == 0, top, total)
+
+        @pl.when(k > 0)
+        def _():
+            for copy in reduce_z(h, k):
+                copy.start()
+
+    def finish(h, send=None):
+        for d in range(1, Z):
+            for copy in reduce_z(h, d):
+                copy.wait_recv()
+        stats = [z_src_stat[h, z]] + [z_stat[h, d] for d in range(1, Z)]
+        numers = [z_src[h, z]] + [z_part[h, d] for d in range(1, Z)]
+        top = stats[0][0:1]
+        for stat in stats[1:]:
+            top = jnp.maximum(top, stat[0:1])
+        total = jnp.zeros((1, QCHIP), jnp.float32)
+        numer = jnp.zeros((HD, QCHIP), jnp.float32)
+        for stat, term in zip(stats, numers):
+            factor = jnp.exp2(stat[0:1] - top)
+            total = total + stat[1:2] * factor
+            numer = numer + term.astype(jnp.float32) * factor
+        mixed = (numer / total).T.astype(jnp.bfloat16)
+        w_rows = pl.ds(pl.multiple_of(h * HD, 32), HD)
+        for place, half in enumerate((1 - x, x)):
+            for part_index in range(2):
+                for at, count in ((0, 512), (512, 384)):
+                    w_cols = pl.ds(
+                        pl.multiple_of(half * COLS + part_index * CHUNK + at, 128), count)
+                    term = jnp.dot(mixed, w_all[w_rows, w_cols], preferred_element_type=jnp.float32)
+                    for c in range(CORES):
+                        acc[half, part_index, c, :, pl.ds(at, count)] += (
+                            term[c * TOK_DEV:(c + 1) * TOK_DEV])
+                if send is not None:
+                    send(place, half, part_index)
+
+    def step(u, par, score, weigh, value):
+        lists = []
+        numer = [None]
+        old_top = tops[2 + par] if value else None
+        if score:
+            h, k = unit_of(u)
+            d = (Z - k) % Z
+            gather_y(h, d).wait_recv()
+
+            @pl.when((k > 0) & (h < HEADS_CORE - 1))
+            def _():
+                forward(h + 1, d)
+
+        if value:
+            lists.append(value_tiles(u - 2, par, numer))
+        if weigh:
+            lists.append(weight_tiles(1 - par))
+        if score:
+            lists.append(score_tiles(u, par))
+        for group in zip(*lists):
+            for work in group:
+                work()
+        if value:
+            h, k = unit_of(u - 2)
+            g = (z + k) % Z
+            for j in range(Y):
+                cols = slice(j * QCHIP, (j + 1) * QCHIP)
+                part[h, g, j] = numer[0][:HD, cols]
+                part_16[h, g, j] = numer[0][:HD, cols].astype(jnp.bfloat16)
+                part_stat[h, g, j] = jnp.where(
+                    tile_row == 0, old_top[:, cols], numer[0][HD:HD + 1, cols])
+            for copy in reduce_y(h, g):
+                copy.start()
+
+    def beside(u):
+        @pl.when((u % Z == 2) & (u < UNITS - Z))
+        def _():
+            prepare_keys(u // Z + 1)
+            prepare_values(u // Z + 1)
+
+        @pl.when(u >= 2 + LAG)
+        def _():
+            merge(u - 2 - LAG)
+
+        @pl.when((u >= 10) & (u % Z == 2))
+        def _():
+            finish((u - 10) // Z)
+
+    arrived(1)
+    arrived(2)
+    prepare_keys(0)
+    for d in range(1, Z):
+        forward(0, d)
+    arrived(3)
+    arrived(4)
+    prepare_values(0)
+    w_copy.wait()
+
+    step(0, 0, True, False, False)
+    step(1, 1, True, True, False)
+
+    @pl.loop(1, UNITS // 2)
+    def _(pair):
+        for par in range(2):
+            step(2 * pair + par, par, True, True, True)
+            beside(2 * pair + par)
+
+    step(UNITS, 0, False, True, True)
+    merge(UNITS - 2 - LAG)
+    step(UNITS + 1, 1, False, False, True)
+    merge(UNITS - 1 - LAG)
+    finish(HEADS_CORE - 2)
+    for u in range(UNITS - LAG, UNITS):
+        merge(u)
+
+    core_out = {}
+
+    def send_core(place, half, part_index):
+        i = place * 2 + part_index
+        core_out[i] = remote(
+            acc.at[half, part_index, 1 - core], c_part.at[place, part_index],
+            o_send.at[i], o_recv.at[i], sibling)
+        core_out[i].start()
+
+    finish(HEADS_CORE - 1, send_core)
+    across = []
+    for i in range(2):
+        core_out[i].wait_recv()
+        x_src[i] = (acc[1 - x, i, core] + c_part[0, i]).astype(jnp.bfloat16)
+        copy = remote(x_src.at[i], x_part.at[i], o_send.at[4 + i], o_recv.at[4 + i], x_peer)
+        copy.start()
+        across.append(copy)
+    for i in range(2):
+        core_out[2 + i].wait_recv()
+        c_part[1, i] = acc[x, i, core] + c_part[1, i]
+    for i in range(2):
+        across[i].wait_recv()
+        out_ref[:, pl.ds(i * CHUNK, CHUNK)] = (
+            c_part[1, i] + x_part[i].astype(jnp.float32)).astype(jnp.bfloat16)
+
+    for copy in core_copies + list(core_out.values()) + across:
+        copy.wait_send()
+
+    @pl.loop(0, HEADS_CORE)
+    def _(h):
+        for d in range(Z):
+            gather_y(h, d).wait_send()
+            for copy in reduce_y(h, d):
+                copy.wait_send()
+            if d > 0:
+                gather_z(h, d).wait_send()
+                for copy in reduce_z(h, d):
+                    copy.wait_send()
+
+
+def fused_shards(
+    queries, new_keys, new_values, key_cache, value_cache, out_weight,
+    cache_len, page_table, block_perm,
+):
+    bf16, f32 = jnp.bfloat16, jnp.float32
+    vmem, dma = pltpu.VMEM, pltpu.SemaphoreType.DMA
+    hc = HEADS_CORE
+    block = (HD, QCHIP)
+    stat = (8, QCHIP)
+    scratch = [
+        vmem((CORES, TOK_DEV, GROUP), bf16),
+        vmem((CORES, TOK_DEV, GROUP), bf16),
+        vmem((CORES, TOK_DEV, GROUP), bf16),
+        vmem((CORES, P_DEV, PAGE, GROUP), bf16),
+        vmem((CORES, P_DEV, PAGE, GROUP), bf16),
+        vmem((GROUP, XS * COLS), bf16),
+        vmem((hc, Z, Y) + block, bf16),
+        vmem((hc, KEYS, HD), bf16),
+        vmem((hc, VROWS, KEYS), bf16),
+        vmem((KEYS, QW), f32),
+        vmem((KEYS, QW), f32),
+        vmem((KEYS, QW), bf16),
+        vmem((KEYS, QW), bf16),
+        vmem((4, 8, QW), f32),
+        vmem((hc, Z, Y) + block, f32),
+        vmem((hc, Z, Y) + block, bf16),
+        vmem((hc, Z, Y) + stat, f32),
+        vmem((hc, Z) + block, bf16),
+        vmem((hc, Z) + stat, f32),
+        vmem((hc, Z) + block, bf16),
+        vmem((hc, Z) + stat, f32),
+        vmem((hc, Z) + block, bf16),
+        vmem((hc, Z) + stat, f32),
+        vmem((XS, 2, CORES, TOK_DEV, CHUNK), f32),
+        vmem((2, 2, TOK_DEV, CHUNK), f32),
+        vmem((2, TOK_DEV, CHUNK), bf16),
+        vmem((2, TOK_DEV, CHUNK), bf16),
+        dma((6,)), dma((5,)), dma((5,)),
+        dma((hc, Z)), dma((hc, Z)), dma((hc, Z)), dma((hc, Z)),
+        dma((hc, Z, 2)), dma((hc, Z, 2)), dma((hc, Z, 2)), dma((hc, Z, 2)),
+        dma((6,)), dma((6,)),
+    ]
+    flops = 4 * hc * Z * QW * KEYS * HD + 2 * QCHIP * GROUP * XS * COLS
+    return pl.pallas_call(
+        fused_kernel,
+        out_shape=jax.ShapeDtypeStruct((TOK_DEV, COLS), bf16),
+        in_specs=[pl.BlockSpec(memory_space=pltpu.SMEM)] + [pl.BlockSpec(memory_space=pl.ANY)] * 6,
+        out_specs=pl.BlockSpec(memory_space=pltpu.VMEM),
+        scratch_shapes=scratch,
+        compiler_params=pltpu.CompilerParams(
+            collective_id=0, has_side_effects=True, vmem_limit_bytes=56 * 1024 * 1024),
+        cost_estimate=pl.CostEstimate(
+            flops=flops, bytes_accessed=14 * 1024 * 1024, transcendentals=hc * Z * QW * KEYS),
+    )(block_perm, queries, new_keys, new_values, key_cache, value_cache, out_weight)
+
+
 def solution(mesh):
     in_specs = (
         P("blk", "head"),
@@ -144,4 +595,5 @@
         P(),
     )
     out_specs = P("blk", "head")
-    return jax.shard_map(shards, mesh=mesh, in_specs=in_specs, out_specs=out_specs, check_vma=False)
+    local = fused_shards if fits_fused(mesh) else shards
+    return jax.shard_map(local, mesh=mesh, in_specs=in_specs, out_specs=out_specs, check_vma=False)

time: 457 us -> 74.2 us (0.16)
  waiting for transfers between devices: 213 us -> 0 us
  local copies, waits for them, and re-layouts: 116 us -> 1.64 us
  Pallas kernels: 0 us -> 72.4 us
  matrix products: 69.3 us -> 0 us
  other arithmetic: 27.3 us -> 0 us
  between operations: 16 us -> 0.01 us
  starting transfers between devices: 13.5 us -> 0 us
    all_to_all x3 -> x0, waiting for transfers between devices: 120 us -> none  [the longest x1 115 us: shards(): lax.all_to_all(send_numer, 'blk', split_axis=0, concat_axis=0, tiled=True)]
    pallas_call x0 -> x1, Pallas kernels: none -> 72.4 us  [fused_shards(): pl.pallas_call(fused_kernel, out_shape=jax.ShapeDtypeStruct((TOK_DEV, COL...]
    dot_general x19 -> x0, matrix products: 69.3 us -> none  [the longest x9 31.3 us: block_partial(): jnp.einsum('qhd,khd->hqk', query_heads, key_heads, preferred_element_type...]
    reduce_scatter x1 -> x0, waiting for transfers between devices: 46.6 us -> none  [shards(): lax.psum_scatter(head_term, 'head', scatter_dimension=1, tiled=True)]
    all_gather x1 -> x0, waiting for transfers between devices: 45.4 us -> none  [shards(): gathered = lax.all_gather(queries, 'blk', axis=0, tiled=True)]
    while x48 -> x0, local copies, waits for them, and re-layouts: 23.8 us -> none
    reshape x8 -> x0, local copies, waits for them, and re-layouts: 21.7 us -> none  [the longest x1 10.5 us: shards(): send_numer = numer_all.reshape(blk_count, TOK_DEV, row_width)[block_perm]]
    dynamic_slice x33 -> x0, local copies, waits for them, and re-layouts: 20.3 us -> none  [the longest x16 11.9 us: page_work(): lax.dynamic_index_in_dim(value_cache, slot_index, 0, keepdims=False)]
  transfers between devices with their start and end apart: 5 -> 0, of which waited for: 4 -> 0; matrix products, arithmetic and copies ran while one was open for 13% -> 0% of each run, Pallas kernels for 0% -> 0%
where the time goes in v2:
time: 74.2 us; the launch traced here: 74 us
  Pallas kernels  72.4 us (98%)
  local copies, waits for them, and re-layouts  1.64 us (2%)
    pallas_call x1, Pallas kernels, fused_shards(): pl.pallas_call(fused_kernel, out_shape=jax.ShapeDtypeStruct((TOK_DEV, COL...  72.4 us
    unnamed x1, local copies, waits for them, and re-layouts  1.64 us

profile of v2, /device:TPU:0, one launch (start us, length us, event | category | flops | bytes accessed | tf_op | source)
XLA Modules:
  0.0 74.0 jit_solution(3580145212563523007)
XLA Ops:
  0.0 72.4 %shard_map.73 = bf16[64,1792]{1,0:T(8,128)(2,1)} custom-call(s32[16]{0:T(128)} %perm.1, bf16[64,1792]{1,0:T(8,128)(2,1)} %q_hbm.1, bf16[64,1792]{1,0:T(8,128)(2,1)} %nk_hbm.1, bf16[64,1792]{1,0:T(8,128)(2,1)} %nv_hbm.1, bf16[8,128,1792]{2,1,0:T(8,128)(2,1)} %kc_hbm.1, bf16[8,128,1792]{2,1,0:T(8,128)(2,1)} %vc_hbm.1, bf16[1792,3584]{1,0:T(8,128)(2,1)} %w_hbm.1), custom_call_target="tpu_custom_call" | custom-call | flops 8808038400 | bytes 14680064 | tf_op jit(solution)/shard_map/pallas_call | solution.py:572
  72.4 1.6 %copy.9 = bf16[64,1792]{1,0:T(8,128)(2,1)} copy(bf16[64,1792]{1,0:T(8,128)(2,1)} %shard_map.73) | data formatting | bytes 458752

commit v3 on v2

--- a/solution.py
+++ b/solution.py
@@ -250,10 +250,13 @@
     q_cols = q_rows.T.astype(jnp.bfloat16)
     for h in range(HEADS_CORE):
         q_t[h, z, y] = q_cols[h * HD:(h + 1) * HD]
-    for h in range(HEADS_CORE):
-        gather_y(h, 0).start()
+
+    def send_queries(h):
         for d in range(1, Z):
             gather_z(h, d).start()
+        gather_y(h, 0).start()
+
+    send_queries(0)
 
     v_t[:, pl.ds(HD, VROWS - HD), :] = jnp.ones((HEADS_CORE, VROWS - HD, KEYS), jnp.bfloat16)
     acc[...] = jnp.zeros(acc.shape, jnp.float32)
@@ -299,7 +302,7 @@
 
     row = lax.broadcasted_iota(jnp.int32, (FRESH, QW), 0)
     lane = lax.broadcasted_iota(jnp.int32, (FRESH, QW), 1)
-    tile_row = lax.broadcasted_iota(jnp.int32, (8, QCHIP), 0)
+    tile_row = lax.broadcasted_iota(jnp.int32, (2, QCHIP), 0)
 
     def unit_of(u):
         h, t = u // Z, u % Z
@@ -414,7 +417,7 @@
     def step(u, par, score, weigh, value):
         lists = []
         numer = [None]
-        old_top = tops[2 + par] if value else None
+        old_top = tops[2 + par][0:1] if value else None
         if score:
             h, k = unit_of(u)
             d = (Z - k) % Z
@@ -423,6 +426,10 @@
             @pl.when((k > 0) & (h < HEADS_CORE - 1))
             def _():
                 forward(h + 1, d)
+
+            @pl.when((k == 1) & (h < HEADS_CORE - 2))
+            def _():
+                send_queries(h + 2)
 
         if value:
             lists.append(value_tiles(u - 2, par, numer))
@@ -464,6 +471,7 @@
     prepare_keys(0)
     for d in range(1, Z):
         forward(0, d)
+    send_queries(1)
     arrived(3)
     arrived(4)
     prepare_values(0)
@@ -534,7 +542,7 @@
     vmem, dma = pltpu.VMEM, pltpu.SemaphoreType.DMA
     hc = HEADS_CORE
     block = (HD, QCHIP)
-    stat = (8, QCHIP)
+    stat = (2, QCHIP)
     scratch = [
         vmem((CORES, TOK_DEV, GROUP), bf16),
         vmem((CORES, TOK_DEV, GROUP), bf16),

time: 74.2 us -> 74.9 us (level)
  no operation moved by 1% of the time
where the time goes in v3:
time: 74.9 us; the launch traced here: 74.8 us
  Pallas kernels  73.1 us (98%)
  local copies, waits for them, and re-layouts  1.64 us (2%)
    pallas_call x1, Pallas kernels, fused_shards(): pl.pallas_call(fused_kernel, out_shape=jax.ShapeDtypeStruct((TOK_DEV, COL...  73.1 us
    unnamed x1, local copies, waits for them, and re-layouts  1.64 us

profile of v3, /device:TPU:0, one launch (start us, length us, event | category | flops | bytes accessed | tf_op | source)
XLA Modules:
  0.0 74.8 jit_solution(5644932544425969899)
XLA Ops:
  0.0 73.1 %shard_map.73 = bf16[64,1792]{1,0:T(8,128)(2,1)} custom-call(s32[16]{0:T(128)} %perm.1, bf16[64,1792]{1,0:T(8,128)(2,1)} %q_hbm.1, bf16[64,1792]{1,0:T(8,128)(2,1)} %nk_hbm.1, bf16[64,1792]{1,0:T(8,128)(2,1)} %nv_hbm.1, bf16[8,128,1792]{2,1,0:T(8,128)(2,1)} %kc_hbm.1, bf16[8,128,1792]{2,1,0:T(8,128)(2,1)} %vc_hbm.1, bf16[1792,3584]{1,0:T(8,128)(2,1)} %w_hbm.1), custom_call_target="tpu_custom_call" | custom-call | flops 8808038400 | bytes 14680064 | tf_op jit(solution)/shard_map/pallas_call | solution.py:580
  73.1 1.6 %copy.9 = bf16[64,1792]{1,0:T(8,128)(2,1)} copy(bf16[64,1792]{1,0:T(8,128)(2,1)} %shard_map.73) | data formatting | bytes 458752

commit v4 on v3

--- a/solution.py
+++ b/solution.py
@@ -314,30 +314,30 @@
         queries = jnp.concatenate([q_t[h, g, 0], q_t[h, g, 1]], axis=1)
         top = [None]
 
-        def cached(i):
+        def rows_from(at):
             tile = jnp.dot(
-                k_heads[h, pl.ds(i * 256, 256), :], queries, preferred_element_type=jnp.float32)
-            scores[par][pl.ds(i * 256, 256), :] = tile
-            tile_top = jnp.max(tile.reshape(32, 8, QW), axis=0)
+                k_heads[h, pl.ds(at, KEYS // 2), :], queries, preferred_element_type=jnp.float32)
+            if at > 0:
+                key_pos = jnp.where(
+                    row < TOK_DEV, perm[blk_of(z, y, 0)], perm[blk_of(z, y, 1)]
+                ) * TOK_DEV + row % TOK_DEV
+                query_blk = jnp.zeros((FRESH, QW), jnp.int32)
+                for j in range(Y * CORES):
+                    query_blk = jnp.where(lane // TOK_DEV == j, perm[g * Y * CORES + j], query_blk)
+                seen = query_blk * TOK_DEV + lane % TOK_DEV >= key_pos
+                tile = jnp.concatenate(
+                    [tile[:CACHED - at], jnp.where(seen, tile[CACHED - at:], -1e30)], axis=0)
+            scores[par][pl.ds(at, KEYS // 2), :] = tile
+            tile_top = jnp.max(tile.reshape(KEYS // 16, 8, QW), axis=0)
             top[0] = tile_top if top[0] is None else jnp.maximum(top[0], tile_top)
-
-        def fresh():
-            key_pos = jnp.where(
-                row < TOK_DEV, perm[blk_of(z, y, 0)], perm[blk_of(z, y, 1)]
-            ) * TOK_DEV + row % TOK_DEV
-            query_blk = jnp.zeros((FRESH, QW), jnp.int32)
-            for j in range(Y * CORES):
-                query_blk = jnp.where(lane // TOK_DEV == j, perm[g * Y * CORES + j], query_blk)
-            seen = query_blk * TOK_DEV + lane % TOK_DEV >= key_pos
-            tile = jnp.dot(
-                k_heads[h, pl.ds(CACHED, FRESH), :], queries, preferred_element_type=jnp.float32)
-            tile = jnp.where(seen, tile, -1e30)
-            scores[par][pl.ds(CACHED, FRESH), :] = tile
-            all_top = jnp.maximum(top[0], jnp.max(tile.reshape(FRESH // 8, 8, QW), axis=0))
-            tops[par] = jnp.broadcast_to(
-                jnp.max(all_top, axis=0, keepdims=True) * LOG2_SCALE, (8, QW))
-
-        return [lambda i=i: cached(i) for i in range(CACHED // 256)] + [fresh]
+            if at > 0:
+                tops[par] = jnp.broadcast_to(
+                    jnp.max(top[0], axis=0, keepdims=True) * LOG2_SCALE, (8, QW))
+
+        steps = [lambda: None] * 9
+        steps[1] = lambda: rows_from(0)
+        steps[5] = lambda: rows_from(KEYS // 2)
+        return steps
 
     def weight_tiles(par):
         top = tops[par][0:1]
@@ -363,8 +363,7 @@
             pass
 
         steps = [nothing] * 9
-        for slot, at, count in ((0, 0, 768), (3, 768, 768), (6, 1536, 640)):
-            steps[slot] = lambda at=at, count=count: add(at, count)
+        steps[0] = lambda: add(0, KEYS)
         return steps
 
     def merge(u):

time: 74.9 us -> 75.6 us (level)
  no operation moved by 1% of the time
where the time goes in v4:
time: 75.6 us; the launch traced here: 75.4 us
  Pallas kernels  73.7 us (97%)
  local copies, waits for them, and re-layouts  1.64 us (2%)
    pallas_call x1, Pallas kernels, fused_shards(): pl.pallas_call(fused_kernel, out_shape=jax.ShapeDtypeStruct((TOK_DEV, COL...  73.7 us
    unnamed x1, local copies, waits for them, and re-layouts  1.64 us

profile of v4, /device:TPU:0, one launch (start us, length us, event | category | flops | bytes accessed | tf_op | source)
XLA Modules:
  0.0 75.4 jit_solution(8141816749654466730)
XLA Ops:
  0.0 73.7 %shard_map.73 = bf16[64,1792]{1,0:T(8,128)(2,1)} custom-call(s32[16]{0:T(128)} %perm.1, bf16[64,1792]{1,0:T(8,128)(2,1)} %q_hbm.1, bf16[64,1792]{1,0:T(8,128)(2,1)} %nk_hbm.1, bf16[64,1792]{1,0:T(8,128)(2,1)} %nv_hbm.1, bf16[8,128,1792]{2,1,0:T(8,128)(2,1)} %kc_hbm.1, bf16[8,128,1792]{2,1,0:T(8,128)(2,1)} %vc_hbm.1, bf16[1792,3584]{1,0:T(8,128)(2,1)} %w_hbm.1), custom_call_target="tpu_custom_call" | custom-call | flops 8808038400 | bytes 14680064 | tf_op jit(solution)/shard_map/pallas_call | solution.py:579
  73.8 1.6 %copy.9 = bf16[64,1792]{1,0:T(8,128)(2,1)} copy(bf16[64,1792]{1,0:T(8,128)(2,1)} %shard_map.73) | data formatting | bytes 458752

commit v5 on v4

--- a/solution.py
+++ b/solution.py
@@ -161,9 +161,9 @@
     q_t, k_heads, v_t, scores_a, scores_b, probs_a, probs_b, tops,
     part, part_16, part_stat, y_part, y_stat,
     z_src, z_src_stat, z_part, z_stat,
-    acc, c_part, x_src, x_part,
+    acc, c_part, x_src, x_part, w_far, w_near, mix_src, mix_in,
     local_sem, core_send, core_recv, gz_send, gz_recv, gy_send, gy_recv,
-    ry_send, ry_recv, rz_send, rz_recv, o_send, o_recv,
+    ry_send, ry_recv, rz_send, rz_recv, o_send, o_recv, w_send, w_recv, m_send, m_recv,
 ):
     me = lax.axis_index("blk")
     x = lax.axis_index("head")
@@ -178,19 +178,21 @@
     sibling = (blk_of(z, y, 1 - core), x)
     y_peer = (blk_of(z, 1 - y, core), x)
     x_peer = (me, 1 - x)
+    x_sibling = (blk_of(z, y, 1 - core), 1 - x)
+    last = HEADS_CORE - 1
 
     def z_to(d):
         return (blk_of((z + d) % Z, y, core), x)
-
-    barrier = pltpu.get_barrier_semaphore()
-    for peer in [sibling, y_peer, x_peer] + [z_to(d) for d in range(1, Z)]:
-        pl.semaphore_signal(barrier, inc=1, device_id=peer, device_id_type=MESH)
-    pl.semaphore_wait(barrier, Z + 2)
 
     def remote(src, dst, send_sem, recv_sem, peer):
         return pltpu.make_async_remote_copy(
             src_ref=src, dst_ref=dst, send_sem=send_sem, recv_sem=recv_sem,
             device_id=peer, device_id_type=MESH)
+
+    barrier = pltpu.get_barrier_semaphore()
+    peers = [sibling, y_peer, x_peer, x_sibling] + [z_to(d) for d in range(1, Z)]
+    for peer in peers:
+        pl.semaphore_signal(barrier, inc=1, device_id=peer, device_id_type=MESH)
 
     mine = pl.ds(pl.multiple_of(core * GROUP, 128), GROUP)
     theirs = pl.ds(pl.multiple_of((1 - core) * GROUP, 128), GROUP)
@@ -201,16 +203,33 @@
     local_copies, core_copies = [], []
     for i, (src, dst) in enumerate(staged):
         lead = (slice(None),) * (len(src.shape) - 1)
+        copy = pltpu.make_async_copy(src.at[lead + (mine,)], dst.at[core], local_sem.at[i])
+        copy.start()
+        local_copies.append(copy)
+
+    pl.semaphore_wait(barrier, len(peers))
+    for i, (src, dst) in enumerate(staged):
+        lead = (slice(None),) * (len(src.shape) - 1)
         copy = remote(
             src.at[lead + (theirs,)], dst.at[core], core_send.at[i], core_recv.at[i], sibling)
         copy.start()
         core_copies.append(copy)
-        copy = pltpu.make_async_copy(src.at[lead + (mine,)], dst.at[core], local_sem.at[i])
-        copy.start()
-        local_copies.append(copy)
     w_copy = pltpu.make_async_copy(
         w_hbm.at[pl.ds(pl.multiple_of(core * GROUP, 128), GROUP), :], w_all, local_sem.at[5])
     w_copy.start()
+    near_row = pl.multiple_of((1 - core) * GROUP + last * HD, 32)
+    near_copy = pltpu.make_async_copy(
+        w_hbm.at[pl.ds(near_row, HD), pl.ds(pl.multiple_of(x * COLS, 128), COLS)],
+        w_near, local_sem.at[6])
+    near_copy.start()
+    far_copies = []
+    for c in range(CORES):
+        copy = remote(
+            w_hbm.at[pl.ds(c * GROUP + last * HD, HD),
+                     pl.ds(pl.multiple_of((1 - x) * COLS, 128), COLS)],
+            w_far.at[c], w_send.at[c], w_recv.at[c], x_peer)
+        copy.start()
+        far_copies.append(copy)
 
     def arrived(i):
         local_copies[i].wait()
@@ -384,7 +403,7 @@
             for copy in reduce_z(h, k):
                 copy.start()
 
-    def finish(h, send=None):
+    def mix(h):
         for d in range(1, Z):
             for copy in reduce_z(h, d):
                 copy.wait_recv()
@@ -399,7 +418,10 @@
             factor = jnp.exp2(stat[0:1] - top)
             total = total + stat[1:2] * factor
             numer = numer + term.astype(jnp.float32) * factor
-        mixed = (numer / total).T.astype(jnp.bfloat16)
+        return (numer / total).T.astype(jnp.bfloat16)
+
+    def finish(h, send=None):
+        mixed = mix(h)
         w_rows = pl.ds(pl.multiple_of(h * HD, 32), HD)
         for place, half in enumerate((1 - x, x)):
             for part_index in range(2):
@@ -471,13 +493,12 @@
     for d in range(1, Z):
         forward(0, d)
     send_queries(1)
+    step(0, 0, True, False, False)
+    step(1, 1, True, True, False)
     arrived(3)
     arrived(4)
     prepare_values(0)
     w_copy.wait()
-
-    step(0, 0, True, False, False)
-    step(1, 1, True, True, False)
 
     @pl.loop(1, UNITS // 2)
     def _(pair):
@@ -489,10 +510,6 @@
     merge(UNITS - 2 - LAG)
     step(UNITS + 1, 1, False, False, True)
     merge(UNITS - 1 - LAG)
-    finish(HEADS_CORE - 2)
-    for u in range(UNITS - LAG, UNITS):
-        merge(u)
-
     core_out = {}
 
     def send_core(place, half, part_index):
@@ -502,7 +519,8 @@
             o_send.at[i], o_recv.at[i], sibling)
         core_out[i].start()
 
-    finish(HEADS_CORE - 1, send_core)
+    finish(last - 1, send_core)
+    merge(UNITS - 2)
     across = []
     for i in range(2):
         core_out[i].wait_recv()
@@ -510,14 +528,58 @@
         copy = remote(x_src.at[i], x_part.at[i], o_send.at[4 + i], o_recv.at[4 + i], x_peer)
         copy.start()
         across.append(copy)
+    merge(UNITS - 1)
     for i in range(2):
         core_out[2 + i].wait_recv()
         c_part[1, i] = acc[x, i, core] + c_part[1, i]
+    near_copy.wait()
+    for copy in far_copies:
+        copy.wait_recv()
+
+    mixed = mix(last)
+    for c in range(CORES):
+        mix_src[c] = jnp.concatenate(
+            [mixed[c * TOK_DEV:(c + 1) * TOK_DEV], jnp.zeros((TOK_DEV, 256 - HD), jnp.bfloat16)],
+            axis=1)
+    mix_copies = []
+    for i, (rows, peer) in enumerate(((core, x_peer), (1 - core, x_sibling), (1 - core, sibling))):
+        copy = remote(mix_src.at[rows], mix_in.at[i], m_send.at[i], m_recv.at[i], peer)
+        copy.start()
+        mix_copies.append(copy)
+
+    spans = ((0, 512), (512, 384), (CHUNK, 512), (CHUNK + 512, 384))
+
+    def add_rows(rows, weight_of):
+        for at, count in spans:
+            i, inner = at // CHUNK, at % CHUNK
+            c_part[1, i, :, pl.ds(inner, count)] += jnp.dot(
+                rows, weight_of(at, count), preferred_element_type=jnp.float32)
+
+    def own_weight(at, count):
+        cols = pl.ds(pl.multiple_of(x * COLS + at, 128), count)
+        return w_all[pl.ds(last * HD, HD), cols]
+
+    add_rows(mix_src[core][:, :HD], own_weight)
     for i in range(2):
         across[i].wait_recv()
-        out_ref[:, pl.ds(i * CHUNK, CHUNK)] = (
-            c_part[1, i] + x_part[i].astype(jnp.float32)).astype(jnp.bfloat16)
-
+        c_part[1, i] += x_part[i].astype(jnp.float32)
+    mix_copies[2].wait_recv()
+    add_rows(mix_in[2][:, :HD], lambda at, count: w_near[:, pl.ds(at, count)])
+    mix_copies[0].wait_recv()
+    mix_copies[1].wait_recv()
+    for at, count in spans:
+        i, inner = at // CHUNK, at % CHUNK
+        same = jnp.dot(
+            mix_in[0][:, :HD], w_far[core, :, pl.ds(at, count)],
+            preferred_element_type=jnp.float32)
+        other = jnp.dot(
+            mix_in[1][:, :HD], w_far[1 - core, :, pl.ds(at, count)],
+            preferred_element_type=jnp.float32)
+        out_ref[:, pl.ds(at, count)] = (
+            c_part[1, i, :, pl.ds(inner, count)] + same + other).astype(jnp.bfloat16)
+
+    for copy in far_copies + mix_copies:
+        copy.wait_send()
     for copy in core_copies + list(core_out.values()) + across:
         copy.wait_send()
 
@@ -570,10 +632,14 @@
         vmem((2, 2, TOK_DEV, CHUNK), f32),
         vmem((2, TOK_DEV, CHUNK), bf16),
         vmem((2, TOK_DEV, CHUNK), bf16),
-        dma((6,)), dma((5,)), dma((5,)),
+        vmem((CORES, HD, COLS), bf16),
+        vmem((HD, COLS), bf16),
+        vmem((CORES, TOK_DEV, 256), bf16),
+        vmem((3, TOK_DEV, 256), bf16),
+        dma((7,)), dma((5,)), dma((5,)),
         dma((hc, Z)), dma((hc, Z)), dma((hc, Z)), dma((hc, Z)),
         dma((hc, Z, 2)), dma((hc, Z, 2)), dma((hc, Z, 2)), dma((hc, Z, 2)),
-        dma((6,)), dma((6,)),
+        dma((6,)), dma((6,)), dma((2,)), dma((2,)), dma((3,)), dma((3,)),
     ]
     flops = 4 * hc * Z * QW * KEYS * HD + 2 * QCHIP * GROUP * XS * COLS
     return pl.pallas_call(

time: 75.6 us -> 72.1 us (0.954)
  Pallas kernels: 73.7 us -> 70.3 us
    pallas_call x1, Pallas kernels: 73.7 us -> 70.3 us  [fused_shards(): pl.pallas_call(fused_kernel, out_shape=jax.ShapeDtypeStruct((TOK_DEV, COL...]
where the time goes in v5:
time: 72.1 us; the launch traced here: 71.9 us
  Pallas kernels  70.3 us (98%)
  local copies, waits for them, and re-layouts  1.64 us (2%)
    pallas_call x1, Pallas kernels, fused_shards(): pl.pallas_call(fused_kernel, out_shape=jax.ShapeDtypeStruct((TOK_DEV, COL...  70.3 us
    unnamed x1, local copies, waits for them, and re-layouts  1.64 us

profile of v5, /device:TPU:0, one launch (start us, length us, event | category | flops | bytes accessed | tf_op | source)
XLA Modules:
  0.0 71.9 jit_solution(4503043897371537560)
XLA Ops:
  0.0 70.3 %shard_map.73 = bf16[64,1792]{1,0:T(8,128)(2,1)} custom-call(s32[16]{0:T(128)} %perm.1, bf16[64,1792]{1,0:T(8,128)(2,1)} %q_hbm.1, bf16[64,1792]{1,0:T(8,128)(2,1)} %nk_hbm.1, bf16[64,1792]{1,0:T(8,128)(2,1)} %nv_hbm.1, bf16[8,128,1792]{2,1,0:T(8,128)(2,1)} %kc_hbm.1, bf16[8,128,1792]{2,1,0:T(8,128)(2,1)} %vc_hbm.1, bf16[1792,3584]{1,0:T(8,128)(2,1)} %w_hbm.1), custom_call_target="tpu_custom_call" | custom-call | flops 8808038400 | bytes 14680064 | tf_op jit(solution)/shard_map/pallas_call | solution.py:645
  70.3 1.6 %copy.9 = bf16[64,1792]{1,0:T(8,128)(2,1)} copy(bf16[64,1792]{1,0:T(8,128)(2,1)} %shard_map.73) | data formatting | bytes 458752

commit v6 on v5

--- a/solution.py
+++ b/solution.py
@@ -147,7 +147,8 @@
 CHUNK = COLS // 2
 WINDOW = 384
 UNITS = HEADS_CORE * Z
-LAG = 2
+LAG = 3
+CUTS = ((0, 256), (256, 256), (512, 256), (768, 128))
 LOG2_SCALE = math.log2(math.e) / math.sqrt(HD)
 
 
@@ -194,46 +195,56 @@
     for peer in peers:
         pl.semaphore_signal(barrier, inc=1, device_id=peer, device_id_type=MESH)
 
-    mine = pl.ds(pl.multiple_of(core * GROUP, 128), GROUP)
-    theirs = pl.ds(pl.multiple_of((1 - core) * GROUP, 128), GROUP)
-    staged = [
-        (q_hbm, q_stage), (kc_hbm, k_stage), (nk_hbm, nk_stage),
-        (vc_hbm, v_stage), (nv_hbm, nv_stage),
-    ]
-    local_copies, core_copies = [], []
-    for i, (src, dst) in enumerate(staged):
+    staged = {"q": (q_hbm, q_stage), "nk": (nk_hbm, nk_stage), "nv": (nv_hbm, nv_stage)}
+    swaps = {}
+
+    def swap(name, src, dst, i, at, count):
         lead = (slice(None),) * (len(src.shape) - 1)
-        copy = pltpu.make_async_copy(src.at[lead + (mine,)], dst.at[core], local_sem.at[i])
-        copy.start()
-        local_copies.append(copy)
+
+        def cut(start):
+            return pl.ds(pl.multiple_of(start * GROUP + at, 128), count)
+
+        here = dst.at[(core,) + lead + (pl.ds(at, count),)]
+        swaps[name] = (
+            pltpu.make_async_copy(src.at[lead + (cut(core),)], here, local_sem.at[i]),
+            remote(src.at[lead + (cut(1 - core),)], here, core_send.at[i], core_recv.at[i], sibling),
+        )
+
+    for i, (name, (src, dst)) in enumerate(staged.items()):
+        swap(name, src, dst, i, 0, GROUP)
+    for i, (at, count) in enumerate(CUTS):
+        swap("k%d" % i, kc_hbm, k_stage, 3 + 2 * i, at, count)
+        swap("v%d" % i, vc_hbm, v_stage, 4 + 2 * i, at, count)
+    for name in ("q", "k0", "nk", "v0", "nv"):
+        swaps[name][0].start()
 
     pl.semaphore_wait(barrier, len(peers))
-    for i, (src, dst) in enumerate(staged):
-        lead = (slice(None),) * (len(src.shape) - 1)
-        copy = remote(
-            src.at[lead + (theirs,)], dst.at[core], core_send.at[i], core_recv.at[i], sibling)
-        copy.start()
-        core_copies.append(copy)
+    for name in ("q", "k0", "nk", "v0", "nv"):
+        swaps[name][1].start()
+
+    def start_swap(*names):
+        for name in names:
+            for copy in swaps[name]:
+                copy.start()
+
     w_copy = pltpu.make_async_copy(
-        w_hbm.at[pl.ds(pl.multiple_of(core * GROUP, 128), GROUP), :], w_all, local_sem.at[5])
-    w_copy.start()
+        w_hbm.at[pl.ds(pl.multiple_of(core * GROUP, 128), GROUP), :], w_all, local_sem.at[11])
     near_row = pl.multiple_of((1 - core) * GROUP + last * HD, 32)
     near_copy = pltpu.make_async_copy(
         w_hbm.at[pl.ds(near_row, HD), pl.ds(pl.multiple_of(x * COLS, 128), COLS)],
-        w_near, local_sem.at[6])
-    near_copy.start()
+        w_near, local_sem.at[12])
     far_copies = []
     for c in range(CORES):
         copy = remote(
             w_hbm.at[pl.ds(c * GROUP + last * HD, HD),
                      pl.ds(pl.multiple_of((1 - x) * COLS, 128), COLS)],
             w_far.at[c], w_send.at[c], w_recv.at[c], x_peer)
-        copy.start()
         far_copies.append(copy)
 
-    def arrived(i):
-        local_copies[i].wait()
-        core_copies[i].wait_recv()
+    def arrived(*names):
+        for name in names:
+            swaps[name][0].wait()
+            swaps[name][1].wait_recv()
 
     def gather_z(h, d):
         block = q_t.at[h, z, y]
@@ -264,7 +275,7 @@
                    rz_send.at[h, d, 1], rz_recv.at[h, d, 1], z_to(d)),
         )
 
-    arrived(0)
+    arrived("q")
     q_rows = jnp.concatenate([q_stage[0], q_stage[1]], axis=0).astype(jnp.float32)
     q_cols = q_rows.T.astype(jnp.bfloat16)
     for h in range(HEADS_CORE):
@@ -281,14 +292,16 @@
     acc[...] = jnp.zeros(acc.shape, jnp.float32)
 
     def head_window(h):
+        if isinstance(h, int) and h == 0:
+            return pl.ds(0, 256), 0, 256
         start = jnp.minimum(h * HD // 128 * 128, GROUP - WINDOW)
-        return pl.ds(pl.multiple_of(start, 128), WINDOW), h * HD - start
+        return pl.ds(pl.multiple_of(start, 128), WINDOW), h * HD - start, WINDOW
 
     def prepare_keys(h):
-        window, offset = head_window(h)
+        window, offset, width = head_window(h)
         pick = jnp.where(
-            lax.broadcasted_iota(jnp.int32, (WINDOW, HD), 0)
-            == lax.broadcasted_iota(jnp.int32, (WINDOW, HD), 1) + offset, 1.0, 0.0
+            lax.broadcasted_iota(jnp.int32, (width, HD), 0)
+            == lax.broadcasted_iota(jnp.int32, (width, HD), 1) + offset, 1.0, 0.0
         ).astype(jnp.bfloat16)
 
         def place(rows, at, count):
@@ -297,15 +310,15 @@
 
         for c in range(CORES):
             for page in range(0, P_DEV, 2):
-                rows = k_stage[c, pl.ds(page, 2), :, window].reshape(2 * PAGE, WINDOW)
+                rows = k_stage[c, pl.ds(page, 2), :, window].reshape(2 * PAGE, width)
                 place(rows, (c * P_DEV + page) * PAGE, 2 * PAGE)
             place(nk_stage[c, :, window], CACHED + c * TOK_DEV, TOK_DEV)
 
     def prepare_values(h):
-        window, offset = head_window(h)
+        window, offset, width = head_window(h)
         pick = jnp.where(
-            lax.broadcasted_iota(jnp.int32, (HD, WINDOW), 1)
-            == lax.broadcasted_iota(jnp.int32, (HD, WINDOW), 0) + offset, 1.0, 0.0
+            lax.broadcasted_iota(jnp.int32, (HD, width), 1)
+            == lax.broadcasted_iota(jnp.int32, (HD, width), 0) + offset, 1.0, 0.0
         ).astype(jnp.bfloat16)
 
         def place(rows, at, count):
@@ -315,7 +328,7 @@
 
         for c in range(CORES):
             for page in range(0, P_DEV, 2):
-                rows = v_stage[c, pl.ds(page, 2), :, window].reshape(2 * PAGE, WINDOW)
+                rows = v_stage[c, pl.ds(page, 2), :, window].reshape(2 * PAGE, width)
                 place(rows, (c * P_DEV + page) * PAGE, 2 * PAGE)
         place(jnp.concatenate([nv_stage[c, :, window] for c in range(CORES)], axis=0), CACHED, FRESH)
 
@@ -474,6 +487,11 @@
                 copy.start()
 
     def beside(u):
+        for i in range(1, HEADS_CORE):
+            @pl.when(u == i * Z - 2)
+            def _():
+                arrived("k%d" % i, "v%d" % i)
+
         @pl.when((u % Z == 2) & (u < UNITS - Z))
         def _():
             prepare_keys(u // Z + 1)
@@ -483,22 +501,29 @@
         def _():
             merge(u - 2 - LAG)
 
+        @pl.when(u == 9)
+        def _():
+            w_copy.wait()
+
         @pl.when((u >= 10) & (u % Z == 2))
         def _():
             finish((u - 10) // Z)
 
-    arrived(1)
-    arrived(2)
+    arrived("k0", "nk")
     prepare_keys(0)
     for d in range(1, Z):
         forward(0, d)
     send_queries(1)
+    start_swap("k1", "v1")
     step(0, 0, True, False, False)
     step(1, 1, True, True, False)
-    arrived(3)
-    arrived(4)
+    arrived("v0", "nv")
     prepare_values(0)
-    w_copy.wait()
+    w_copy.start()
+    start_swap("k2", "v2", "k3", "v3")
+    near_copy.start()
+    for copy in far_copies:
+        copy.start()
 
     @pl.loop(1, UNITS // 2)
     def _(pair):
@@ -519,6 +544,7 @@
             o_send.at[i], o_recv.at[i], sibling)
         core_out[i].start()
 
+    merge(UNITS - 3)
     finish(last - 1, send_core)
     merge(UNITS - 2)
     across = []
@@ -580,7 +606,7 @@
 
     for copy in far_copies + mix_copies:
         copy.wait_send()
-    for copy in core_copies + list(core_out.values()) + across:
+    for copy in [pair[1] for pair in swaps.values()] + list(core_out.values()) + across:
         copy.wait_send()
 
     @pl.loop(0, HEADS_CORE)
@@ -636,7 +662,7 @@
         vmem((HD, COLS), bf16),
         vmem((CORES, TOK_DEV, 256), bf16),
         vmem((3, TOK_DEV, 256), bf16),
-        dma((7,)), dma((5,)), dma((5,)),
+        dma((13,)), dma((11,)), dma((11,)),
         dma((hc, Z)), dma((hc, Z)), dma((hc, Z)), dma((hc, Z)),
         dma((hc, Z, 2)), dma((hc, Z, 2)), dma((hc, Z, 2)), dma((hc, Z, 2)),
         dma((6,)), dma((6,)), dma((2,)), dma((2,)), dma((3,)), dma((3,)),

time: 72.1 us -> 73.1 us (1.014)
  Pallas kernels: 70.3 us -> 71.3 us
    pallas_call x1, Pallas kernels: 70.3 us -> 71.3 us  [fused_shards(): pl.pallas_call(fused_kernel, out_shape=jax.ShapeDtypeStruct((TOK_DEV, COL...]
where the time goes in v6:
time: 73.1 us; the launch traced here: 73 us
  Pallas kernels  71.3 us (98%)
  local copies, waits for them, and re-layouts  1.64 us (2%)
    pallas_call x1, Pallas kernels, fused_shards(): pl.pallas_call(fused_kernel, out_shape=jax.ShapeDtypeStruct((TOK_DEV, COL...  71.3 us
    unnamed x1, local copies, waits for them, and re-layouts  1.64 us

profile of v6, /device:TPU:0, one launch (start us, length us, event | category | flops | bytes accessed | tf_op | source)
XLA Modules:
  0.0 73.0 jit_solution(17356484476125481448)
XLA Ops:
  0.0 71.3 %shard_map.73 = bf16[64,1792]{1,0:T(8,128)(2,1)} custom-call(s32[16]{0:T(128)} %perm.1, bf16[64,1792]{1,0:T(8,128)(2,1)} %q_hbm.1, bf16[64,1792]{1,0:T(8,128)(2,1)} %nk_hbm.1, bf16[64,1792]{1,0:T(8,128)(2,1)} %nv_hbm.1, bf16[8,128,1792]{2,1,0:T(8,128)(2,1)} %kc_hbm.1, bf16[8,128,1792]{2,1,0:T(8,128)(2,1)} %vc_hbm.1, bf16[1792,3584]{1,0:T(8,128)(2,1)} %w_hbm.1), custom_call_target="tpu_custom_call" | custom-call | flops 8808038400 | bytes 14680064 | tf_op jit(solution)/shard_map/pallas_call | solution.py:671
  71.3 1.6 %copy.9 = bf16[64,1792]{1,0:T(8,128)(2,1)} copy(bf16[64,1792]{1,0:T(8,128)(2,1)} %shard_map.73) | data formatting | bytes 458752

commit v7 on v5

--- a/solution.py
+++ b/solution.py
@@ -275,7 +275,8 @@
             gather_z(h, d).start()
         gather_y(h, 0).start()
 
-    send_queries(0)
+    for h in range(HEADS_CORE):
+        send_queries(h)
 
     v_t[:, pl.ds(HD, VROWS - HD), :] = jnp.ones((HEADS_CORE, VROWS - HD, KEYS), jnp.bfloat16)
     acc[...] = jnp.zeros(acc.shape, jnp.float32)
@@ -447,10 +448,6 @@
             @pl.when((k > 0) & (h < HEADS_CORE - 1))
             def _():
                 forward(h + 1, d)
-
-            @pl.when((k == 1) & (h < HEADS_CORE - 2))
-            def _():
-                send_queries(h + 2)
 
         if value:
             lists.append(value_tiles(u - 2, par, numer))
@@ -492,7 +489,6 @@
     prepare_keys(0)
     for d in range(1, Z):
         forward(0, d)
-    send_queries(1)
     step(0, 0, True, False, False)
     step(1, 1, True, True, False)
     arrived(3)

time: 72.1 us -> 71.2 us (0.988)
  Pallas kernels: 70.3 us -> 69.4 us
    pallas_call x1, Pallas kernels: 70.3 us -> 69.4 us  [fused_shards(): pl.pallas_call(fused_kernel, out_shape=jax.ShapeDtypeStruct((TOK_DEV, COL...]
where the time goes in v7:
time: 71.2 us; the launch traced here: 71.1 us
  Pallas kernels  69.4 us (97%)
  local copies, waits for them, and re-layouts  1.64 us (2%)
    pallas_call x1, Pallas kernels, fused_shards(): pl.pallas_call(fused_kernel, out_shape=jax.ShapeDtypeStruct((TOK_DEV, COL...  69.4 us
    unnamed x1, local copies, waits for them, and re-layouts  1.64 us

profile of v7, /device:TPU:0, one launch (start us, length us, event | category | flops | bytes accessed | tf_op | source)
XLA Modules:
  0.0 71.1 jit_solution(11914075206451793214)
XLA Ops:
  0.0 69.4 %shard_map.73 = bf16[64,1792]{1,0:T(8,128)(2,1)} custom-call(s32[16]{0:T(128)} %perm.1, bf16[64,1792]{1,0:T(8,128)(2,1)} %q_hbm.1, bf16[64,1792]{1,0:T(8,128)(2,1)} %nk_hbm.1, bf16[64,1792]{1,0:T(8,128)(2,1)} %nv_hbm.1, bf16[8,128,1792]{2,1,0:T(8,128)(2,1)} %kc_hbm.1, bf16[8,128,1792]{2,1,0:T(8,128)(2,1)} %vc_hbm.1, bf16[1792,3584]{1,0:T(8,128)(2,1)} %w_hbm.1), custom_call_target="tpu_custom_call" | custom-call | flops 8808038400 | bytes 14680064 | tf_op jit(solution)/shard_map/pallas_call | solution.py:641
  69.4 1.6 %copy.9 = bf16[64,1792]{1,0:T(8,128)(2,1)} copy(bf16[64,1792]{1,0:T(8,128)(2,1)} %shard_map.73) | data formatting | bytes 458752
